TPU v7x, 128 devices: a whole 4x4x4 slice. The times are simulated.
128 devices in a mesh: dom: 16 (over y, x), grp: 8 (over z, core).
Axes of the slice: x: 4, y: 4, z: 4, core: 2. Of those that a mesh axis runs over, the one named last changes fastest.
Arguments:
- modal_state: float32 [5, 8, 8, 8, 32768], P(None, None, None, None, ('dom', 'grp')), may hold values from -3 to 3
- velocity: float32 [3, 32768], P(None, ('dom', 'grp')), may hold values from -0.5 to 1
- density: float32 [32768], P(('dom', 'grp')), may hold values from 0.5 to 2
- sound_speed: float32 [32768], P(('dom', 'grp')), may hold values from 0.7 to 1.4
- stretch_first: float32 [16], P('dom'), may hold values from 1 to 4
- stretch_second: float32 [8], P('grp'), may hold values from 1 to 4
- stretch_third: float32 [256], replicated, may hold values from 1 to 4
- orders: int32 [256], P(('dom', 'grp')), may hold values from 3 to 7, as said below
Outputs:
- advanced: float32 [5, 8, 8, 8, 32768], P(None, None, None, None, ('dom', 'grp'))
Inputs may be any that keep to these rules, and one draw needn't show every extreme that they name: `orders`: each tile of 128 consecutive elements carries one order.
All inputs are finite; a program needn't handle non-finite values.
Results may differ from a plain program's by a relative error of at most 0.0001.
Values sent between devices are 32-bit elements; how exact they have to be, the bound alone decides.
No kernel may reach another device: no remote copies, remote signals or barrier semaphores. Data moves between devices by JAX's collectives and lax.ppermute only.
A program may use at most 64 MiB of HBM per device.

v0:
```python
import functools

import jax
import jax.numpy as jnp
from jax import lax
from jax.experimental import pallas as pl
from jax.experimental.pallas import tpu as pltpu
from jax.sharding import PartitionSpec as P

HALF_WAVE = 1.25
TIME_STEP = 0.01
SECTION_A2 = -0.4178904745
SECTION_B1 = 0.1496590219993
SECTION_B2 = 0.3792103129999
MODES = 8
FIELDS = 5
LANES = 128
TILES = 2
FACE = (TILES, FIELDS, MODES * MODES, LANES)
BULK = (TILES, FIELDS, MODES, MODES * MODES, LANES)
F32 = jnp.float32
VMEM_LIMIT = 24 * 1024 * 1024


def rows(m):
    if isinstance(m, int):
        return pl.ds(m * MODES, MODES)
    return pl.ds(pl.multiple_of(m * MODES, MODES), MODES)


def strided(m):
    return pl.ds(m, MODES, stride=MODES)


def flux(q, d, u, rho, inv, stiff):
    n = q[1 + d]
    out = [u * q[0] + rho * n, u * q[1], u * q[2], u * q[3], u * q[4] + stiff * n]
    out[1 + d] = out[1 + d] + inv * q[4]
    return out


def wide(ref, row, t):
    return jnp.broadcast_to(ref[row : row + 1, t * LANES : (t + 1) * LANES], (MODES, LANES))


def medium(vel, den, snd, t):
    rho = wide(den, 0, t)
    c = wide(snd, 0, t)
    return [wide(vel, k, t) for k in range(3)], rho, 1.0 / rho, rho * c * c


def levels(order):
    third = lax.broadcasted_iota(jnp.int32, (MODES, LANES), 0)
    return [jnp.where(jnp.maximum(third, k) <= order, 1.0, 0.0).astype(F32) for k in range(MODES)]


def place():
    out = []
    for axis in ("dom", "grp"):
        i = lax.axis_index(axis)
        n = lax.axis_size(axis)
        sign = (1 - 2 * lax.rem(i, 2)).astype(F32)
        has = jnp.logical_and(i > 0, i < n - 1)
        out.append((sign, has))
    return out


def write_faces(d, sign, coef, even_of, odd_of, slots, t):
    us, rho, inv, stiff = coef
    half = 0.5 * sign
    u = half * us[d]
    near, far = HALF_WAVE + u, HALF_WAVE - u
    rho, inv, stiff = half * rho, half * inv, half * stiff
    for m in range(MODES):
        even, odd = even_of(m), odd_of(m)
        odd = [sign * a for a in odd]
        one = flux([a + b for a, b in zip(even, odd)], d, near, rho, inv, stiff)
        two = flux([a - b for a, b in zip(even, odd)], d, far, -rho, -inv, -stiff)
        for f in range(FIELDS):
            slots[0][t, f, rows(m), :] = one[f]
            slots[1][t, f, rows(m), :] = two[f]


def halo_pair(slots, sign, has, t, f, m, scale):
    near = slots[0][t, f, rows(m), :]
    far = jnp.where(has, slots[1][t, f, rows(m), :], 0.0)
    return scale * (near + far), (scale * sign) * (near - far)


def first_faces(orders, vel, den, snd, modal, q0, x_even, x_odd, y_even, y_odd, sums, sems):
    copies = {}
    for t in range(TILES):
        for f in range(FIELDS):
            copies[t, f] = pltpu.make_async_copy(
                modal.at[f, :, :, pl.ds(t * LANES, LANES)], q0.at[t, f], sems.at[t, f]
            )
            copies[t, f].start()
    (sign_x, _), (sign_y, _) = place()
    for t in range(TILES):
        mask = levels(orders[t])
        for f in range(FIELDS):
            copies[t, f].wait()
            e0 = [None] * MODES
            o0 = [None] * MODES
            for a in range(MODES):
                e1 = o1 = None
                for b in range(MODES):
                    q = mask[max(a, b)] * q0[t, f, a, rows(b), :]
                    q0[t, f, a, rows(b), :] = q
                    if a % 2 == 0:
                        e0[b] = q if e0[b] is None else e0[b] + q
                    else:
                        o0[b] = q if o0[b] is None else o0[b] + q
                    if b % 2 == 0:
                        e1 = q if e1 is None else e1 + q
                    else:
                        o1 = q if o1 is None else o1 + q
                sums[2, f, rows(a), :] = e1
                sums[3, f, rows(a), :] = o1
            for b in range(MODES):
                sums[0, f, rows(b), :] = e0[b]
                sums[1, f, rows(b), :] = o0[b]
        coef = medium(vel, den, snd, t)
        for d, sign, slots in ((0, sign_x, (x_even, x_odd)), (1, sign_y, (y_even, y_odd))):
            write_faces(
                d,
                sign,
                coef,
                lambda m: [sums[2 * d, f, rows(m), :] for f in range(FIELDS)],
                lambda m: [sums[2 * d + 1, f, rows(m), :] for f in range(FIELDS)],
                slots,
                t,
            )


def scaled(coef, d, s):
    us, rho, inv, stiff = coef
    return s * us[d], s * rho, s * inv, s * stiff


def bases(d, even, odd, us, k):
    a_odd = flux(odd, d, *us)
    a_even = flux(even, d, *us)
    return (
        [-0.5 * (x + k * e) for x, e in zip(a_odd, even)],
        [-0.5 * (x + k * o) for x, o in zip(a_even, odd)],
    )


def parity_sums(load):
    even, odd = load(0), load(1)
    for m in range(2, MODES, 2):
        even = [a + b for a, b in zip(even, load(m))]
        odd = [a + b for a, b in zip(odd, load(m + 1))]
    return even, odd


def sweep(d, load, even, odd, us, emit):
    run = [even, odd]
    for m in range(MODES):
        here = run[m % 2]
        emit(m, [(2.0 * m + 1.0) * a for a in here] if m else here)
        if m < MODES - 1:
            w = flux(load(m), d, *us)
            run[1 - m % 2] = [a + b for a, b in zip(run[1 - m % 2], w)]


def third_direction(q, acc, coefs, g2, h):
    lane = lax.broadcasted_iota(jnp.int32, (MODES, LANES), 1)
    first, last = lane == 0, lane == LANES - 1

    def line(a, carry):
        def loader(t):
            return lambda m: [q[t, f, a, strided(m), :] for f in range(FIELDS)]

        own, up, down = [], [], []
        for t in range(TILES):
            even, odd = parity_sums(loader(t))
            own.append((even, odd))
            us, rho, inv, stiff = coefs[t]
            u = 0.5 * us[2]
            rho, inv, stiff = 0.5 * rho, 0.5 * inv, 0.5 * stiff
            upper = flux([x + y for x, y in zip(even, odd)], 2, HALF_WAVE + u, rho, inv, stiff)
            lower = flux([x - y for x, y in zip(even, odd)], 2, HALF_WAVE - u, -rho, -inv, -stiff)
            up.append([pltpu.roll(x, 1, 1) for x in upper])
            down.append([pltpu.roll(x, LANES - 1, 1) for x in lower])
        for t in range(TILES):
            s = h * g2[t]
            half = 0.5 * s
            us = scaled(coefs[t], 2, s)
            base_e, base_o = bases(2, *own[t], us, 2.0 * HALF_WAVE * s)
            for f in range(FIELDS):
                prior = jnp.where(first, up[1 - t][f], up[t][f])
                after = jnp.where(last, down[1 - t][f], down[t][f])
                base_e[f] = base_e[f] + half * (after + prior)
                base_o[f] = base_o[f] + half * (after - prior)

            def emit(m, terms):
                for f in range(FIELDS):
                    acc[t, f, a, strided(m), :] = terms[f]

            sweep(2, loader(t), base_e, base_o, us, emit)
        return carry

    lax.fori_loop(0, MODES, line, 0)


def second_direction(q, acc, coefs, g1, h):
    s = h * g1
    for t in range(TILES):
        us = scaled(coefs[t], 1, s)

        def line(a, carry):
            def load(m):
                return [q[t, f, a, rows(m), :] for f in range(FIELDS)]

            even, odd = parity_sums(load)
            base_e, base_o = bases(1, even, odd, us, 2.0 * HALF_WAVE * s)

            def emit(m, terms):
                for f in range(FIELDS):
                    acc[t, f, a, rows(m), :] = acc[t, f, a, rows(m), :] + terms[f]

            sweep(1, load, base_e, base_o, us, emit)
            return carry

        lax.fori_loop(0, MODES, line, 0)


def first_direction(q, acc, coefs, g0, h, finish):
    s = h * g0
    for t in range(TILES):
        us = scaled(coefs[t], 0, s)

        def line(b, carry):
            def load(m):
                return [q[t, f, m, rows(b), :] for f in range(FIELDS)]

            even, odd = parity_sums(load)
            base_e, base_o = bases(0, even, odd, us, 2.0 * HALF_WAVE * s)

            def emit(m, terms):
                finish(t, m, b, [acc[t, f, m, rows(b), :] + terms[f] for f in range(FIELDS)])

            sweep(0, load, base_e, base_o, us, emit)
            return carry

        lax.fori_loop(0, MODES, line, 0)


def store_levels(orders, mask_ref):
    for t in range(TILES):
        for k, level in enumerate(levels(orders[t])):
            mask_ref[t, k] = level


def local_rate(orders, g0, g1, vel, den, snd, g2_ref, q0, r1, traces, acc, mask_ref):
    coefs = [medium(vel, den, snd, t) for t in range(TILES)]
    g2 = [wide(g2_ref, 0, t) for t in range(TILES)]
    store_levels(orders, mask_ref)
    traces[...] = jnp.zeros(traces.shape, F32)
    third_direction(q0, acc, coefs, g2, TIME_STEP)
    second_direction(q0, acc, coefs, g1[0], TIME_STEP)

    def finish(t, a, b, totals):
        level = mask_ref[t, jnp.maximum(a, b)]
        slot = 2 + lax.rem(b, 2)
        for f in range(FIELDS):
            rate = level * totals[f]
            r1[t, f, a, rows(b), :] = rate
            q = q0[t, f, a, rows(b), :] + SECTION_B1 * rate
            traces[a % 2, t, f, rows(b), :] = traces[a % 2, t, f, rows(b), :] + q
            traces[slot, t, f, rows(a), :] = traces[slot, t, f, rows(a), :] + q

    first_direction(q0, acc, coefs, g0[0], TIME_STEP, finish)


def second_faces(
    orders, g0, g1, vel, den, snd, traces, xe, xo, ye, yo, x_even, x_odd, y_even, y_odd, face
):
    (sign_x, has_x), (sign_y, has_y) = place()
    for t in range(TILES):
        order = orders[t]
        mask = levels(order)
        weights = [
            sum(jnp.where(m <= order, m + 0.5, 0.0) for m in range(parity, MODES, 2)) for parity in range(2)
        ]
        scale = (SECTION_B1 * TIME_STEP * g0[0], SECTION_B1 * TIME_STEP * g1[0])
        for f in range(FIELDS):
            pairs = []
            across = []
            for d, slots, sign, has in ((0, (xe, xo), sign_x, has_x), (1, (ye, yo), sign_y, has_y)):
                pair = [halo_pair(slots, sign, has, t, f, m, scale[d]) for m in range(MODES)]
                pairs.append(pair)
                across.append(
                    [
                        [sum(mask[m] * pair[m][kind] for m in range(parity, MODES, 2)) for parity in range(2)]
                        for kind in range(2)
                    ]
                )
            for d in range(2):
                for m in range(MODES):
                    for parity in range(2):
                        add = weights[parity] * pairs[d][m][parity] + (m + 0.5) * across[1 - d][m % 2][parity]
                        face[2 * d + parity, f, rows(m), :] = (
                            traces[2 * d + parity, t, f, rows(m), :] + mask[m] * add
                        )
        coef = medium(vel, den, snd, t)
        for d, sign, slots in ((0, sign_x, (x_even, x_odd)), (1, sign_y, (y_even, y_odd))):
            write_faces(
                d,
                sign,
                coef,
                lambda m: [face[2 * d, f, rows(m), :] for f in range(FIELDS)],
                lambda m: [face[2 * d + 1, f, rows(m), :] for f in range(FIELDS)],
                slots,
                t,
            )


def store_halos(halo, xe, xo, ye, yo, scale_x, scale_y):
    (sign_x, has_x), (sign_y, has_y) = place()
    for d, slots, sign, has, scale in ((0, (xe, xo), sign_x, has_x, scale_x), (1, (ye, yo), sign_y, has_y, scale_y)):
        for t in range(TILES):

            def one(f, carry):
                for m in range(MODES):
                    plus, minus = halo_pair(slots, sign, has, t, f, m, scale)
                    halo[d, 0, t, f, rows(m), :] = plus
                    halo[d, 1, t, f, rows(m), :] = minus
                return carry

            lax.fori_loop(0, FIELDS, one, 0)


def halo_term(halo, t, f, a, b, weight, kind):
    return (a + 0.5) * halo[0, a % 2, t, f, rows(b), :] + weight * halo[1, kind, t, f, rows(a), :]


def second_local(
    orders, g0, g1, vel, den, snd, g2_ref, q0, r1, xe, xo, ye, yo, part, q1, acc, halo, mask_ref
):
    coefs = [medium(vel, den, snd, t) for t in range(TILES)]
    g2 = [wide(g2_ref, 0, t) for t in range(TILES)]
    store_levels(orders, mask_ref)
    store_halos(halo, xe, xo, ye, yo, TIME_STEP * g0[0], TIME_STEP * g1[0])
    for t in range(TILES):

        def column(b, carry):
            weight = b.astype(F32) + 0.5
            kind = lax.rem(b, 2)
            for a in range(MODES):
                level = mask_ref[t, jnp.maximum(a, b)]
                for f in range(FIELDS):
                    rate = r1[t, f, a, rows(b), :] + level * halo_term(halo, t, f, a, b, weight, kind)
                    q = q0[t, f, a, rows(b), :] + SECTION_B1 * rate
                    q1[t, f, a, rows(b), :] = q
                    part[t, f, a, rows(b), :] = q + (SECTION_B2 * SECTION_A2) * rate
            return carry

        lax.fori_loop(0, MODES, column, 0)
    third_direction(q1, acc, coefs, g2, SECTION_B2 * TIME_STEP)
    second_direction(q1, acc, coefs, g1[0], SECTION_B2 * TIME_STEP)

    def finish(t, a, b, totals):
        level = mask_ref[t, jnp.maximum(a, b)]
        for f in range(FIELDS):
            part[t, f, a, rows(b), :] = part[t, f, a, rows(b), :] + level * totals[f]

    first_direction(q1, acc, coefs, g0[0], SECTION_B2 * TIME_STEP, finish)


def last_add(orders, g0, g1, part, xe, xo, ye, yo, out, done, halo, sems):
    s = SECTION_B2 * TIME_STEP
    store_halos(halo, xe, xo, ye, yo, s * g0[0], s * g1[0])
    copies = []
    for t in range(TILES):
        mask = levels(orders[t])
        for f in range(FIELDS):
            for a in range(MODES):
                for b in range(MODES):
                    term = halo_term(halo, t, f, a, b, b + 0.5, b % 2)
                    done[t, f, a, rows(b), :] = part[t, f, a, rows(b), :] + mask[max(a, b)] * term
            copy = pltpu.make_async_copy(done.at[t, f], out.at[f, :, :, pl.ds(t * LANES, LANES)], sems.at[t, f])
            copy.start()
            copies.append(copy)
    for copy in copies:
        copy.wait()


SCALAR = pl.BlockSpec(memory_space=pltpu.SMEM)
LOCAL = pl.BlockSpec(memory_space=pltpu.VMEM)
ANYWHERE = pl.BlockSpec(memory_space=pl.ANY)


def call(body, operands, specs, outs, out_specs, scratch, cost):
    return pl.pallas_call(
        body,
        out_shape=outs,
        in_specs=specs,
        out_specs=out_specs,
        scratch_shapes=scratch,
        compiler_params=pltpu.CompilerParams(vmem_limit_bytes=VMEM_LIMIT),
        cost_estimate=pl.CostEstimate(flops=cost, bytes_accessed=2_600_000, transcendentals=0),
        name=body.__name__,
    )(*operands)


def exchange(dom_perms, grp_perms, faces):
    x_even, x_odd, y_even, y_odd = faces
    both = ("dom", "grp")
    return (
        lax.ppermute(x_even, "dom", dom_perms[0]),
        lax.ppermute(x_odd, both, dom_perms[1]),
        lax.ppermute(y_even, "grp", grp_perms[0]),
        lax.ppermute(y_odd, "grp", grp_perms[1]),
    )


def pair_swaps(n_dom, n_grp):
    even = lambda n: [(i, i ^ 1) for i in range(n)]
    other = lambda i: ((i - 1) ^ 1) + 1
    dom_odd = []
    for i in range(n_dom):
        for j in range(n_grp):
            if 0 < i < n_dom - 1:
                target = other(i) * n_grp + j
            else:
                target = i * n_grp + (j ^ 1)
            dom_odd.append((i * n_grp + j, target))
    grp_odd = [(j, other(j) if 0 < j < n_grp - 1 else n_grp - 1 - j) for j in range(n_grp)]
    return (even(n_dom), dom_odd), (even(n_grp), grp_odd)


def per_device(n_dom, n_grp, modal, vel, den, snd, g0, g1, g2, orders):
    dom_perms, grp_perms = pair_swaps(n_dom, n_grp)
    swap = functools.partial(exchange, dom_perms, grp_perms)
    shape = modal.shape
    modal = modal.reshape(FIELDS, MODES, MODES * MODES, TILES * LANES)
    den, snd, g2 = (x.reshape(1, TILES * LANES) for x in (den, snd, g2))
    face = jax.ShapeDtypeStruct(FACE, F32)
    bulk = jax.ShapeDtypeStruct(BULK, F32)
    sems = pltpu.SemaphoreType.DMA((TILES, FIELDS))
    plane = (FIELDS, MODES * MODES, LANES)
    q0, *faces = call(
        first_faces,
        (orders, vel, den, snd, modal),
        [SCALAR, LOCAL, LOCAL, LOCAL, ANYWHERE],
        (bulk,) + (face,) * 4,
        (LOCAL,) * 5,
        [pltpu.VMEM((4,) + plane, F32), sems],
        2_000_000,
    )
    halos = swap(faces)
    masks = pltpu.VMEM((TILES, MODES, MODES, LANES), F32)
    r1, traces = call(
        local_rate,
        (orders, g0, g1, vel, den, snd, g2, q0),
        [SCALAR] * 3 + [LOCAL] * 5,
        (bulk, jax.ShapeDtypeStruct((4,) + FACE, F32)),
        (LOCAL,) * 2,
        [pltpu.VMEM(BULK, F32), masks],
        16_000_000,
    )
    faces = call(
        second_faces,
        (orders, g0, g1, vel, den, snd, traces, *halos),
        [SCALAR] * 3 + [LOCAL] * 8,
        (face,) * 4,
        (LOCAL,) * 4,
        [pltpu.VMEM((4,) + plane, F32)],
        2_000_000,
    )
    last = swap(faces)
    halo = pltpu.VMEM((2, 2) + FACE, F32)
    part = call(
        second_local,
        (orders, g0, g1, vel, den, snd, g2, q0, r1, *halos),
        [SCALAR] * 3 + [LOCAL] * 10,
        bulk,
        LOCAL,
        [pltpu.VMEM(BULK, F32), pltpu.VMEM(BULK, F32), halo, masks],
        20_000_000,
    )
    out = call(
        last_add,
        (orders, g0, g1, part, *last),
        [SCALAR] * 3 + [LOCAL] * 5,
        jax.ShapeDtypeStruct(modal.shape, F32),
        ANYWHERE,
        [pltpu.VMEM(BULK, F32), halo, sems],
        4_000_000,
    )
    return out.reshape(shape)


def solution(mesh):
    placed = (
        P(None, None, None, None, ("dom", "grp")),
        P(None, ("dom", "grp")),
        P(("dom", "grp")),
        P(("dom", "grp")),
        P("dom"),
        P("grp"),
        P(),
        P(("dom", "grp")),
    )
    return jax.shard_map(
        functools.partial(per_device, mesh.shape["dom"], mesh.shape["grp"]),
        mesh=mesh,
        in_specs=placed,
        out_specs=P(None, None, None, None, ("dom", "grp")),
        check_vma=False,
    )
```

profile of v0, /device:TPU:24, one launch (start us, length us, event | category | flops | bytes accessed | tf_op | source)
XLA Modules:
  0.0 35.7 jit_solution(3949090169050055324)
XLA Ops:
  0.0 0.0 copy-start.6
  0.0 0.0 copy-start
  0.0 1.8 %copy-done = f32[5,8,8,8,256]{4,3,2,1,0:T(8,128)S(1)} copy-done((f32[5,8,8,8,256]{4,3,2,1,0:T(8,128)S(1)}, f32[5,8,8,8,256]{4,3,2,1,0:T(8,128)}, u32[]{:S(2)}) %copy-start) | copy-done | bytes 2621464
  1.8 0.0 copy-start.1
  1.8 0.7 %copy-done.1 = f32[3,256]{1,0:T(4,128)S(1)} copy-done((f32[3,256]{1,0:T(4,128)S(1)}, f32[3,256]{1,0:T(4,128)}, u32[]{:S(2)}) %copy-start.1) | copy-done | bytes 3096
  2.4 0.0 copy-start.2
  2.4 0.7 %copy-done.2 = f32[256]{0:T(256)S(1)} copy-done((f32[256]{0:T(256)S(1)}, f32[256]{0:T(256)}, u32[]{:S(2)}) %copy-start.2) | copy-done | bytes 1048
  3.1 0.0 copy-start.3
  3.1 0.7 %copy-done.3 = f32[256]{0:T(256)S(1)} copy-done((f32[256]{0:T(256)S(1)}, f32[256]{0:T(256)}, u32[]{:S(2)}) %copy-start.3) | copy-done | bytes 1048
  3.8 0.0 copy-start.5
  3.8 0.7 %copy-done.5 = s32[2]{0:T(128)S(1)} copy-done((s32[2]{0:T(128)S(1)}, s32[2]{0:T(128)}, u32[]{:S(2)}) %copy-start.5) | copy-done | bytes 32
  4.5 1.3 %first_faces.1 = (f32[2,5,8,64,128]{4,3,2,1,0:T(8,128)S(1)}, f32[2,5,64,128]{3,2,1,0:T(8,128)S(1)}, f32[2,5,64,128]{3,2,1,0:T(8,128)S(1)}, f32[2,5,64,128]{3,2,1,0:T(8,128)S(1)}, f32[2,5,64,128]{3,2,1,0:T(8,128)S(1)}) custom-call(s32[2]{0:T(128)S(1)} %copy-done.5, f32[3,256]{1,0:T(4,128)S(1)} %copy-done.1, f32[1,256]{1,0:T(1,128)S(1)} %bitcast.6, ...), custom_call_target="tpu_custom_call" | custom-call | flops 2000000 | bytes 2600000 | tf_op jit(solution)/shard_map/first_faces/pallas_call | solution.py:397
  5.8 1.6 %collective-permute-start = (f32[2,5,64,128]{3,2,1,0:T(8,128)S(1)}, f32[2,5,64,128]{3,2,1,0:T(8,128)S(1)}, u32[]{:S(2)}, u32[]{:S(2)}) collective-permute-start(f32[2,5,64,128]{3,2,1,0:T(8,128)S(1)} %get-tuple-element.18), channel_id=1, source_target_pairs={{0,8},{8,0},{16,24},{24,16},{32,40},{40,32},{48,56},{56,48},{64,72... | collective-permute-start | bytes 983048 | tf_op jit(solution)/shard_map/ppermute | solution.py:413
  7.4 2.3 %collective-permute-start.1 = (f32[2,5,64,128]{3,2,1,0:T(8,128)S(1)}, f32[2,5,64,128]{3,2,1,0:T(8,128)S(1)}, u32[]{:S(2)}, u32[]{:S(2)}) collective-permute-start(f32[2,5,64,128]{3,2,1,0:T(8,128)S(1)} %get-tuple-element.19), channel_id=1, source_target_pairs={{0,1},{1,0},{2,3},{3,2},{4,5},{5,4},{6,7},{7,6},{8,16},{9,17},{10,... | collective-permute-start | bytes 983048 | tf_op jit(solution)/shard_map/ppermute | solution.py:414
  9.6 0.0 collective-permute-start.2
  9.6 4.1 %collective-permute-start.3 = (f32[2,5,64,128]{3,2,1,0:T(8,128)S(1)}, f32[2,5,64,128]{3,2,1,0:T(8,128)S(1)}, u32[]{:S(2)}, u32[]{:S(2)}) collective-permute-start(f32[2,5,64,128]{3,2,1,0:T(8,128)S(1)} %get-tuple-element.21), channel_id=1, source_target_pairs={{0,7},{1,2},{2,1},{3,4},{4,3},{5,6},{6,5},{7,0},{8,15},{9,10},{10,... | collective-permute-start | bytes 983048 | tf_op jit(solution)/shard_map/ppermute | solution.py:416
  15.1 0.0 copy-done.6
  15.1 0.0 copy-start.4
  15.1 7.2 %local_rate.1 = (f32[2,5,8,64,128]{4,3,2,1,0:T(8,128)S(1)}, f32[4,2,5,64,128]{4,3,2,1,0:T(8,128)S(1)}) custom-call(s32[2]{0:T(128)S(1)} %copy-done.5, f32[1]{0:T(128)S(6)} %copy.9.g0, f32[1]{0:T(128)S(6)} %copy.10.g1, f32[3,256]{1,0:T(4,128)S(1)} %copy-done.1, f32[1,256]{1,0:T(1,128)S(1)} %bitcast.7, f32[1,256]{1,0:T(1,128)S(1)} %bitcast.11, ...), custom_call_target="tpu_custom_call" | custom-call | flops 16000000 | bytes 2600000 | tf_op jit(solution)/shard_map/local_rate/pallas_call | solution.py:397
  22.3 0.0 collective-permute-done.xe
  22.3 0.0 collective-permute-done.1.xo
  22.3 0.0 collective-permute-done.2.ye
  22.3 0.0 collective-permute-done.3.yo
  22.3 1.1 %second_faces.1 = (f32[2,5,64,128]{3,2,1,0:T(8,128)S(1)}, f32[2,5,64,128]{3,2,1,0:T(8,128)S(1)}, f32[2,5,64,128]{3,2,1,0:T(8,128)S(1)}, f32[2,5,64,128]{3,2,1,0:T(8,128)S(1)}) custom-call(s32[2]{0:T(128)S(1)} %copy-done.5, f32[1]{0:T(128)S(6)} %copy.9.g0, f32[1]{0:T(128)S(6)} %copy.10.g1, f32[3,256]{1,0:T(4,128)S(1)} %copy-done.1, f32[1,256]{1,0:T(1,128)S(1)} %bitcast.8, ...), custom_call_target="tpu_custom_call" | custom-call | flops 2000000 | bytes 2600000 | tf_op jit(solution)/shard_map/second_faces/pallas_call | solution.py:397
  23.5 0.5 %collective-permute-start.4 = (f32[2,5,64,128]{3,2,1,0:T(8,128)S(1)}, f32[2,5,64,128]{3,2,1,0:T(8,128)S(1)}, u32[]{:S(2)}, u32[]{:S(2)}) collective-permute-start(f32[2,5,64,128]{3,2,1,0:T(8,128)S(1)} %get-tuple-element.23), channel_id=1, source_target_pairs={{0,8},{8,0},{16,24},{24,16},{32,40},{40,32},{48,56},{56,48},{64,72... | collective-permute-start | bytes 983048 | tf_op jit(solution)/shard_map/ppermute | solution.py:413
  24.0 1.5 %collective-permute-start.5 = (f32[2,5,64,128]{3,2,1,0:T(8,128)S(1)}, f32[2,5,64,128]{3,2,1,0:T(8,128)S(1)}, u32[]{:S(2)}, u32[]{:S(2)}) collective-permute-start(f32[2,5,64,128]{3,2,1,0:T(8,128)S(1)} %get-tuple-element.24), channel_id=1, source_target_pairs={{0,1},{1,0},{2,3},{3,2},{4,5},{5,4},{6,7},{7,6},{8,16},{9,17},{10,... | collective-permute-start | bytes 983048 | tf_op jit(solution)/shard_map/ppermute | solution.py:414
  25.5 0.0 collective-permute-start.6
  25.5 0.9 %collective-permute-start.7 = (f32[2,5,64,128]{3,2,1,0:T(8,128)S(1)}, f32[2,5,64,128]{3,2,1,0:T(8,128)S(1)}, u32[]{:S(2)}, u32[]{:S(2)}) collective-permute-start(f32[2,5,64,128]{3,2,1,0:T(8,128)S(1)} %get-tuple-element.26), channel_id=1, source_target_pairs={{0,7},{1,2},{2,1},{3,4},{4,3},{5,6},{6,5},{7,0},{8,15},{9,10},{10,... | collective-permute-start | bytes 983048 | tf_op jit(solution)/shard_map/ppermute | solution.py:416
  26.4 0.0 copy-done.4
  26.4 5.2 %second_local.1.part = f32[2,5,8,64,128]{4,3,2,1,0:T(8,128)S(1)} custom-call(s32[2]{0:T(128)S(1)} %copy-done.5, f32[1]{0:T(128)S(6)} %copy.9.g0, f32[1]{0:T(128)S(6)} %copy.10.g1, f32[3,256]{1,0:T(4,128)S(1)} %copy-done.1, f32[1,256]{1,0:T(1,128)S(1)} %bitcast.9, f32[1,256]{1,0:T(1,128)S(1)} %bitcast.13, f32[1,256]{1,0:T(1,128)S(1)} %bitcast.15, ...), custom_call_target="tpu_custom_call" | custom-call | flops 20000000 | bytes 2600000 | tf_op jit(solution)/shard_map/second_local/pallas_call | solution.py:397
  31.6 0.0 collective-permute-done.4.xe
  31.6 1.7 %collective-permute-done.5.xo = f32[2,5,64,128]{3,2,1,0:T(8,128)S(1)} collective-permute-done((f32[2,5,64,128]{3,2,1,0:T(8,128)S(1)}, f32[2,5,64,128]{3,2,1,0:T(8,128)S(1)}, u32[]{:S(2)}, u32[]{:S(2)}) %collective-permute-start.5) | collective-permute-done | bytes 327712 | tf_op jit(solution)/shard_map/ppermute | solution.py:414
  33.3 0.0 collective-permute-done.6.ye
  33.3 0.0 collective-permute-done.7.yo
  33.3 2.4 %last_add.1 = f32[5,8,64,256]{3,2,1,0:T(8,128)} custom-call(s32[2]{0:T(128)S(1)} %copy-done.5, f32[1]{0:T(128)S(6)} %copy.9.g0, f32[1]{0:T(128)S(6)} %copy.10.g1, f32[2,5,8,64,128]{4,3,2,1,0:T(8,128)S(1)} %second_local.1.part, f32[2,5,64,128]{3,2,1,0:T(8,128)S(1)} %collective-permute-done.4.xe, f32[2,5,64,128]{3,2,1,0:T(8,128)S(1)} %collective-permute-done.5.xo, ...), custom_call_target="tpu_custom_call" | custom-call | flops 4000000 | bytes 2600000 | tf_op jit(solution)/shard_map/last_add/pallas_call | solution.py:397
Async XLA Ops:
  0.0 15.1 %copy-start.6 = (f32[256]{0:T(256)S(1)}, f32[256]{0:T(256)}, u32[]{:S(2)}) copy-start(f32[256]{0:T(256)} %param.14) | copy-start | bytes 3076
  0.0 1.8 %copy-start = (f32[5,8,8,8,256]{4,3,2,1,0:T(8,128)S(1)}, f32[5,8,8,8,256]{4,3,2,1,0:T(8,128)}, u32[]{:S(2)}) copy-start(f32[5,8,8,8,256]{4,3,2,1,0:T(8,128)} %param.8) | copy-start | bytes 7864324
  1.8 0.7 %copy-start.1 = (f32[3,256]{1,0:T(4,128)S(1)}, f32[3,256]{1,0:T(4,128)}, u32[]{:S(2)}) copy-start(f32[3,256]{1,0:T(4,128)} %vel.7) | copy-start | bytes 9220
  2.4 0.7 %copy-start.2 = (f32[256]{0:T(256)S(1)}, f32[256]{0:T(256)}, u32[]{:S(2)}) copy-start(f32[256]{0:T(256)} %param.10) | copy-start | bytes 3076
  3.1 0.7 %copy-start.3 = (f32[256]{0:T(256)S(1)}, f32[256]{0:T(256)}, u32[]{:S(2)}) copy-start(f32[256]{0:T(256)} %param.11) | copy-start | bytes 3076
  3.8 0.7 %copy-start.5 = (s32[2]{0:T(128)S(1)}, s32[2]{0:T(128)}, u32[]{:S(2)}) copy-start(s32[2]{0:T(128)} %orders.9) | copy-start | bytes 28
  5.8 16.5 %collective-permute-start = (f32[2,5,64,128]{3,2,1,0:T(8,128)S(1)}, f32[2,5,64,128]{3,2,1,0:T(8,128)S(1)}, u32[]{:S(2)}, u32[]{:S(2)}) collective-permute-start(f32[2,5,64,128]{3,2,1,0:T(8,128)S(1)} %get-tuple-element.18), channel_id=1, source_target_pairs={{0,8},{8,0},{16,24},{24,16},{32,40},{40,32},{48,56},{56,48},{64,72... | collective-permute-start | bytes 983048 | tf_op jit(solution)/shard_map/ppermute | solution.py:413
  7.4 14.9 %collective-permute-start.1 = (f32[2,5,64,128]{3,2,1,0:T(8,128)S(1)}, f32[2,5,64,128]{3,2,1,0:T(8,128)S(1)}, u32[]{:S(2)}, u32[]{:S(2)}) collective-permute-start(f32[2,5,64,128]{3,2,1,0:T(8,128)S(1)} %get-tuple-element.19), channel_id=1, source_target_pairs={{0,1},{1,0},{2,3},{3,2},{4,5},{5,4},{6,7},{7,6},{8,16},{9,17},{10,... | collective-permute-start | bytes 983048 | tf_op jit(solution)/shard_map/ppermute | solution.py:414
  9.6 12.7 %collective-permute-start.2 = (f32[2,5,64,128]{3,2,1,0:T(8,128)S(1)}, f32[2,5,64,128]{3,2,1,0:T(8,128)S(1)}, u32[]{:S(2)}, u32[]{:S(2)}) collective-permute-start(f32[2,5,64,128]{3,2,1,0:T(8,128)S(1)} %get-tuple-element.20), channel_id=1, source_target_pairs={{0,1},{1,0},{2,3},{3,2},{4,5},{5,4},{6,7},{7,6},{8,9},{9,8},{10,11... | collective-permute-start | bytes 983048 | tf_op jit(solution)/shard_map/ppermute | solution.py:415
  9.6 12.7 %collective-permute-start.3 = (f32[2,5,64,128]{3,2,1,0:T(8,128)S(1)}, f32[2,5,64,128]{3,2,1,0:T(8,128)S(1)}, u32[]{:S(2)}, u32[]{:S(2)}) collective-permute-start(f32[2,5,64,128]{3,2,1,0:T(8,128)S(1)} %get-tuple-element.21), channel_id=1, source_target_pairs={{0,7},{1,2},{2,1},{3,4},{4,3},{5,6},{6,5},{7,0},{8,15},{9,10},{10,... | collective-permute-start | bytes 983048 | tf_op jit(solution)/shard_map/ppermute | solution.py:416
  15.1 11.3 %copy-start.4 = (f32[256]{0:T(256)S(1)}, f32[256]{0:T(256)}, u32[]{:S(2)}) copy-start(f32[256]{0:T(256)} %param.11) | copy-start | bytes 3076
  23.5 8.1 %collective-permute-start.4 = (f32[2,5,64,128]{3,2,1,0:T(8,128)S(1)}, f32[2,5,64,128]{3,2,1,0:T(8,128)S(1)}, u32[]{:S(2)}, u32[]{:S(2)}) collective-permute-start(f32[2,5,64,128]{3,2,1,0:T(8,128)S(1)} %get-tuple-element.23), channel_id=1, source_target_pairs={{0,8},{8,0},{16,24},{24,16},{32,40},{40,32},{48,56},{56,48},{64,72... | collective-permute-start | bytes 983048 | tf_op jit(solution)/shard_map/ppermute | solution.py:413
  24.0 9.3 %collective-permute-start.5 = (f32[2,5,64,128]{3,2,1,0:T(8,128)S(1)}, f32[2,5,64,128]{3,2,1,0:T(8,128)S(1)}, u32[]{:S(2)}, u32[]{:S(2)}) collective-permute-start(f32[2,5,64,128]{3,2,1,0:T(8,128)S(1)} %get-tuple-element.24), channel_id=1, source_target_pairs={{0,1},{1,0},{2,3},{3,2},{4,5},{5,4},{6,7},{7,6},{8,16},{9,17},{10,... | collective-permute-start | bytes 983048 | tf_op jit(solution)/shard_map/ppermute | solution.py:414
  25.5 7.8 %collective-permute-start.6 = (f32[2,5,64,128]{3,2,1,0:T(8,128)S(1)}, f32[2,5,64,128]{3,2,1,0:T(8,128)S(1)}, u32[]{:S(2)}, u32[]{:S(2)}) collective-permute-start(f32[2,5,64,128]{3,2,1,0:T(8,128)S(1)} %get-tuple-element.25), channel_id=1, source_target_pairs={{0,1},{1,0},{2,3},{3,2},{4,5},{5,4},{6,7},{7,6},{8,9},{9,8},{10,11... | collective-permute-start | bytes 983048 | tf_op jit(solution)/shard_map/ppermute | solution.py:415
  25.5 7.8 %collective-permute-start.7 = (f32[2,5,64,128]{3,2,1,0:T(8,128)S(1)}, f32[2,5,64,128]{3,2,1,0:T(8,128)S(1)}, u32[]{:S(2)}, u32[]{:S(2)}) collective-permute-start(f32[2,5,64,128]{3,2,1,0:T(8,128)S(1)} %get-tuple-element.26), channel_id=1, source_target_pairs={{0,7},{1,2},{2,1},{3,4},{4,3},{5,6},{6,5},{7,0},{8,15},{9,10},{10,... | collective-permute-start | bytes 983048 | tf_op jit(solution)/shard_map/ppermute | solution.py:416
where the time goes:
time: 35.9 us; the launch traced here: 35.7 us
  Pallas kernels  17.2 us (48%)
  starting transfers between devices  10.9 us (30%)
  local copies, waits for them, and re-layouts  4.46 us (12%)
  waiting for transfers between devices  1.68 us (5%)
  between operations  1.39 us (4%)
    pallas_call x5, Pallas kernels, call(): pl.pallas_call(body, out_shape=outs, in_specs=specs, out_specs=out_specs,...  17.2 us
    ppermute x2, starting transfers between devices, exchange(): lax.ppermute(y_odd, 'grp', grp_perms[1])  5.04 us
    unnamed x14, local copies, waits for them, and re-layouts  4.46 us
    ppermute x2, starting transfers between devices, exchange(): lax.ppermute(x_odd, both, dom_perms[1])  3.82 us
    ppermute x2, starting transfers between devices, exchange(): lax.ppermute(x_even, 'dom', dom_perms[0])  2.06 us
    ppermute x2, waiting for transfers between devices, exchange(): lax.ppermute(x_odd, both, dom_perms[1])  1.67 us
  transfers between devices with their start and end apart: 8, of which 1 were waited for; matrix products, arithmetic and copies ran while one was open for 0% of the time, Pallas kernels for 35%

commit v1 on v0

--- a/solution.py
+++ b/solution.py
@@ -39,19 +39,37 @@
     return out
 
 
-def wide(ref, row, t):
-    return jnp.broadcast_to(ref[row : row + 1, t * LANES : (t + 1) * LANES], (MODES, LANES))
-
-
-def medium(vel, den, snd, t):
-    rho = wide(den, 0, t)
-    c = wide(snd, 0, t)
-    return [wide(vel, k, t) for k in range(3)], rho, 1.0 / rho, rho * c * c
-
-
-def levels(order):
+FLOW, RHO, INVERSE, STIFF, THIRD, LEVEL, WEIGHT = 0, 3, 4, 5, 6, 7, 15
+COEFS = (TILES, 17, MODES, LANES)
+
+
+def spread(ref, t, row=0):
+    lanes = pl.ds(t * LANES, LANES)
+    part = ref[lanes].reshape(1, -1) if len(ref.shape) == 1 else ref[pl.ds(row, 1), lanes]
+    return jnp.broadcast_to(part, (MODES, LANES))
+
+
+def store_coefs(coefs, vel, den, snd, g2, orders):
     third = lax.broadcasted_iota(jnp.int32, (MODES, LANES), 0)
-    return [jnp.where(jnp.maximum(third, k) <= order, 1.0, 0.0).astype(F32) for k in range(MODES)]
+    for t in range(TILES):
+        for k in range(3):
+            coefs[t, FLOW + k] = spread(vel, t, k)
+        rho, c = spread(den, t), spread(snd, t)
+        coefs[t, RHO] = rho
+        coefs[t, INVERSE] = 1.0 / rho
+        coefs[t, STIFF] = rho * c * c
+        coefs[t, THIRD] = spread(g2, t)
+        order = jnp.broadcast_to(orders[pl.ds(t, 1)].reshape(1, 1), (MODES, LANES))
+        for k in range(MODES):
+            coefs[t, LEVEL + k] = jnp.where(jnp.maximum(third, k) <= order, 1.0, 0.0).astype(F32)
+        for parity in range(2):
+            coefs[t, WEIGHT + parity] = sum(
+                jnp.where(order >= m, m + 0.5, 0.0).astype(F32) for m in range(parity, MODES, 2)
+            )
+
+
+def medium(coefs, t):
+    return [coefs[t, FLOW + k] for k in range(3)], coefs[t, RHO], coefs[t, INVERSE], coefs[t, STIFF]
 
 
 def place():
@@ -87,7 +105,11 @@
     return scale * (near + far), (scale * sign) * (near - far)
 
 
-def first_faces(orders, vel, den, snd, modal, q0, x_even, x_odd, y_even, y_odd, sums, sems):
+def first_faces(*refs):
+    small, (modal, q0, coefs, x_even, x_odd, y_even, y_odd), (sums, sems, *held, small_sems) = refs[:5], refs[5:12], refs[12:]
+    loads = [pltpu.make_async_copy(a, b, small_sems.at[i]) for i, (a, b) in enumerate(zip(small, held))]
+    for load in loads:
+        load.start()
     copies = {}
     for t in range(TILES):
         for f in range(FIELDS):
@@ -96,8 +118,10 @@
             )
             copies[t, f].start()
     (sign_x, _), (sign_y, _) = place()
-    for t in range(TILES):
-        mask = levels(orders[t])
+    for load in loads:
+        load.wait()
+    store_coefs(coefs, *held)
+    for t in range(TILES):
         for f in range(FIELDS):
             copies[t, f].wait()
             e0 = [None] * MODES
@@ -105,7 +129,7 @@
             for a in range(MODES):
                 e1 = o1 = None
                 for b in range(MODES):
-                    q = mask[max(a, b)] * q0[t, f, a, rows(b), :]
+                    q = coefs[t, LEVEL + max(a, b)] * q0[t, f, a, rows(b), :]
                     q0[t, f, a, rows(b), :] = q
                     if a % 2 == 0:
                         e0[b] = q if e0[b] is None else e0[b] + q
@@ -120,7 +144,7 @@
             for b in range(MODES):
                 sums[0, f, rows(b), :] = e0[b]
                 sums[1, f, rows(b), :] = o0[b]
-        coef = medium(vel, den, snd, t)
+        coef = medium(coefs, t)
         for d, sign, slots in ((0, sign_x, (x_even, x_odd)), (1, sign_y, (y_even, y_odd))):
             write_faces(
                 d,
@@ -165,7 +189,7 @@
             run[1 - m % 2] = [a + b for a, b in zip(run[1 - m % 2], w)]
 
 
-def third_direction(q, acc, coefs, g2, h):
+def third_direction(q, acc, coefs, metric, h):
     lane = lax.broadcasted_iota(jnp.int32, (MODES, LANES), 1)
     first, last = lane == 0, lane == LANES - 1
 
@@ -177,7 +201,7 @@
         for t in range(TILES):
             even, odd = parity_sums(loader(t))
             own.append((even, odd))
-            us, rho, inv, stiff = coefs[t]
+            us, rho, inv, stiff = medium(coefs, t)
             u = 0.5 * us[2]
             rho, inv, stiff = 0.5 * rho, 0.5 * inv, 0.5 * stiff
             upper = flux([x + y for x, y in zip(even, odd)], 2, HALF_WAVE + u, rho, inv, stiff)
@@ -185,9 +209,9 @@
             up.append([pltpu.roll(x, 1, 1) for x in upper])
             down.append([pltpu.roll(x, LANES - 1, 1) for x in lower])
         for t in range(TILES):
-            s = h * g2[t]
+            s = h * coefs[t, THIRD]
             half = 0.5 * s
-            us = scaled(coefs[t], 2, s)
+            us = scaled(medium(coefs, t), 2, s)
             base_e, base_o = bases(2, *own[t], us, 2.0 * HALF_WAVE * s)
             for f in range(FIELDS):
                 prior = jnp.where(first, up[1 - t][f], up[t][f])
@@ -205,10 +229,10 @@
     lax.fori_loop(0, MODES, line, 0)
 
 
-def second_direction(q, acc, coefs, g1, h):
-    s = h * g1
-    for t in range(TILES):
-        us = scaled(coefs[t], 1, s)
+def second_direction(q, acc, coefs, metric, h):
+    for t in range(TILES):
+        s = h * metric[1]
+        us = scaled(medium(coefs, t), 1, s)
 
         def line(a, carry):
             def load(m):
@@ -227,10 +251,10 @@
         lax.fori_loop(0, MODES, line, 0)
 
 
-def first_direction(q, acc, coefs, g0, h, finish):
-    s = h * g0
-    for t in range(TILES):
-        us = scaled(coefs[t], 0, s)
+def first_direction(q, acc, coefs, metric, h, finish):
+    for t in range(TILES):
+        s = h * metric[0]
+        us = scaled(medium(coefs, t), 0, s)
 
         def line(b, carry):
             def load(m):
@@ -239,8 +263,10 @@
             even, odd = parity_sums(load)
             base_e, base_o = bases(0, even, odd, us, 2.0 * HALF_WAVE * s)
 
+            kept = {}
+
             def emit(m, terms):
-                finish(t, m, b, [acc[t, f, m, rows(b), :] + terms[f] for f in range(FIELDS)])
+                finish(t, b, m, [acc[t, f, m, rows(b), :] + terms[f] for f in range(FIELDS)], kept)
 
             sweep(0, load, base_e, base_o, us, emit)
             return carry
@@ -248,44 +274,35 @@
         lax.fori_loop(0, MODES, line, 0)
 
 
-def store_levels(orders, mask_ref):
-    for t in range(TILES):
-        for k, level in enumerate(levels(orders[t])):
-            mask_ref[t, k] = level
-
-
-def local_rate(orders, g0, g1, vel, den, snd, g2_ref, q0, r1, traces, acc, mask_ref):
-    coefs = [medium(vel, den, snd, t) for t in range(TILES)]
-    g2 = [wide(g2_ref, 0, t) for t in range(TILES)]
-    store_levels(orders, mask_ref)
-    traces[...] = jnp.zeros(traces.shape, F32)
-    third_direction(q0, acc, coefs, g2, TIME_STEP)
-    second_direction(q0, acc, coefs, g1[0], TIME_STEP)
-
-    def finish(t, a, b, totals):
-        level = mask_ref[t, jnp.maximum(a, b)]
+def local_rate(coefs, g0, g1, q0, r1, traces, acc):
+    metric = g0[0], g1[0]
+    traces[pl.ds(2, 2)] = jnp.zeros((2,) + FACE, F32)
+    third_direction(q0, acc, coefs, metric, TIME_STEP)
+    second_direction(q0, acc, coefs, metric, TIME_STEP)
+
+    def finish(t, b, a, totals, kept):
+        level = coefs[t, LEVEL + jnp.maximum(a, b)]
         slot = 2 + lax.rem(b, 2)
         for f in range(FIELDS):
             rate = level * totals[f]
             r1[t, f, a, rows(b), :] = rate
             q = q0[t, f, a, rows(b), :] + SECTION_B1 * rate
-            traces[a % 2, t, f, rows(b), :] = traces[a % 2, t, f, rows(b), :] + q
+            kept[a % 2, f] = q if a < 2 else kept[a % 2, f] + q
             traces[slot, t, f, rows(a), :] = traces[slot, t, f, rows(a), :] + q
-
-    first_direction(q0, acc, coefs, g0[0], TIME_STEP, finish)
-
-
-def second_faces(
-    orders, g0, g1, vel, den, snd, traces, xe, xo, ye, yo, x_even, x_odd, y_even, y_odd, face
-):
+        if a == MODES - 1:
+            for (parity, f), total in kept.items():
+                traces[parity, t, f, rows(b), :] = total
+
+    first_direction(q0, acc, coefs, metric, TIME_STEP, finish)
+
+
+def second_faces(coefs, g0, g1, traces, xe, xo, ye, yo, x_even, x_odd, y_even, y_odd, face):
+    metric = g0[0], g1[0]
     (sign_x, has_x), (sign_y, has_y) = place()
     for t in range(TILES):
-        order = orders[t]
-        mask = levels(order)
-        weights = [
-            sum(jnp.where(m <= order, m + 0.5, 0.0) for m in range(parity, MODES, 2)) for parity in range(2)
-        ]
-        scale = (SECTION_B1 * TIME_STEP * g0[0], SECTION_B1 * TIME_STEP * g1[0])
+        mask = [coefs[t, LEVEL + k] for k in range(MODES)]
+        weights = [coefs[t, WEIGHT + parity] for parity in range(2)]
+        scale = [SECTION_B1 * TIME_STEP * metric[d] for d in range(2)]
         for f in range(FIELDS):
             pairs = []
             across = []
@@ -305,7 +322,7 @@
                         face[2 * d + parity, f, rows(m), :] = (
                             traces[2 * d + parity, t, f, rows(m), :] + mask[m] * add
                         )
-        coef = medium(vel, den, snd, t)
+        coef = medium(coefs, t)
         for d, sign, slots in ((0, sign_x, (x_even, x_odd)), (1, sign_y, (y_even, y_odd))):
             write_faces(
                 d,
@@ -318,10 +335,11 @@
             )
 
 
-def store_halos(halo, xe, xo, ye, yo, scale_x, scale_y):
+def store_halos(halo, xe, xo, ye, yo, metric, s):
     (sign_x, has_x), (sign_y, has_y) = place()
-    for d, slots, sign, has, scale in ((0, (xe, xo), sign_x, has_x, scale_x), (1, (ye, yo), sign_y, has_y, scale_y)):
+    for d, slots, sign, has in ((0, (xe, xo), sign_x, has_x), (1, (ye, yo), sign_y, has_y)):
         for t in range(TILES):
+            scale = s * metric[d]
 
             def one(f, carry):
                 for m in range(MODES):
@@ -337,20 +355,16 @@
     return (a + 0.5) * halo[0, a % 2, t, f, rows(b), :] + weight * halo[1, kind, t, f, rows(a), :]
 
 
-def second_local(
-    orders, g0, g1, vel, den, snd, g2_ref, q0, r1, xe, xo, ye, yo, part, q1, acc, halo, mask_ref
-):
-    coefs = [medium(vel, den, snd, t) for t in range(TILES)]
-    g2 = [wide(g2_ref, 0, t) for t in range(TILES)]
-    store_levels(orders, mask_ref)
-    store_halos(halo, xe, xo, ye, yo, TIME_STEP * g0[0], TIME_STEP * g1[0])
+def second_local(coefs, g0, g1, q0, r1, xe, xo, ye, yo, part, q1, acc, halo):
+    metric = g0[0], g1[0]
+    store_halos(halo, xe, xo, ye, yo, metric, TIME_STEP)
     for t in range(TILES):
 
         def column(b, carry):
             weight = b.astype(F32) + 0.5
             kind = lax.rem(b, 2)
             for a in range(MODES):
-                level = mask_ref[t, jnp.maximum(a, b)]
+                level = coefs[t, LEVEL + jnp.maximum(a, b)]
                 for f in range(FIELDS):
                     rate = r1[t, f, a, rows(b), :] + level * halo_term(halo, t, f, a, b, weight, kind)
                     q = q0[t, f, a, rows(b), :] + SECTION_B1 * rate
@@ -359,23 +373,23 @@
             return carry
 
         lax.fori_loop(0, MODES, column, 0)
-    third_direction(q1, acc, coefs, g2, SECTION_B2 * TIME_STEP)
-    second_direction(q1, acc, coefs, g1[0], SECTION_B2 * TIME_STEP)
-
-    def finish(t, a, b, totals):
-        level = mask_ref[t, jnp.maximum(a, b)]
+    third_direction(q1, acc, coefs, metric, SECTION_B2 * TIME_STEP)
+    second_direction(q1, acc, coefs, metric, SECTION_B2 * TIME_STEP)
+
+    def finish(t, b, a, totals, kept):
+        level = coefs[t, LEVEL + jnp.maximum(a, b)]
         for f in range(FIELDS):
             part[t, f, a, rows(b), :] = part[t, f, a, rows(b), :] + level * totals[f]
 
-    first_direction(q1, acc, coefs, g0[0], SECTION_B2 * TIME_STEP, finish)
-
-
-def last_add(orders, g0, g1, part, xe, xo, ye, yo, out, done, halo, sems):
-    s = SECTION_B2 * TIME_STEP
-    store_halos(halo, xe, xo, ye, yo, s * g0[0], s * g1[0])
+    first_direction(q1, acc, coefs, metric, SECTION_B2 * TIME_STEP, finish)
+
+
+def last_add(coefs, g0, g1, part, xe, xo, ye, yo, out, done, halo, sems):
+    metric = g0[0], g1[0]
+    store_halos(halo, xe, xo, ye, yo, metric, SECTION_B2 * TIME_STEP)
     copies = []
     for t in range(TILES):
-        mask = levels(orders[t])
+        mask = [coefs[t, LEVEL + k] for k in range(MODES)]
         for f in range(FIELDS):
             for a in range(MODES):
                 for b in range(MODES):
@@ -390,7 +404,7 @@
 
 SCALAR = pl.BlockSpec(memory_space=pltpu.SMEM)
 LOCAL = pl.BlockSpec(memory_space=pltpu.VMEM)
-ANYWHERE = pl.BlockSpec(memory_space=pl.ANY)
+FAR = pl.BlockSpec(memory_space=pltpu.HBM)
 
 
 def call(body, operands, specs, outs, out_specs, scratch, cost):
@@ -437,35 +451,36 @@
     swap = functools.partial(exchange, dom_perms, grp_perms)
     shape = modal.shape
     modal = modal.reshape(FIELDS, MODES, MODES * MODES, TILES * LANES)
-    den, snd, g2 = (x.reshape(1, TILES * LANES) for x in (den, snd, g2))
+    small = [vel, den, snd, g2, orders]
     face = jax.ShapeDtypeStruct(FACE, F32)
     bulk = jax.ShapeDtypeStruct(BULK, F32)
     sems = pltpu.SemaphoreType.DMA((TILES, FIELDS))
     plane = (FIELDS, MODES * MODES, LANES)
-    q0, *faces = call(
+    q0, coefs, *faces = call(
         first_faces,
-        (orders, vel, den, snd, modal),
-        [SCALAR, LOCAL, LOCAL, LOCAL, ANYWHERE],
-        (bulk,) + (face,) * 4,
-        (LOCAL,) * 5,
-        [pltpu.VMEM((4,) + plane, F32), sems],
+        tuple(pltpu.with_memory_space_constraint(x, pltpu.HBM) for x in (*small, modal)),
+        [FAR] * 6,
+        (bulk, jax.ShapeDtypeStruct(COEFS, F32)) + (face,) * 4,
+        (LOCAL,) * 6,
+        [pltpu.VMEM((4,) + plane, F32), sems]
+        + [pltpu.VMEM(x.shape, x.dtype) for x in small]
+        + [pltpu.SemaphoreType.DMA((len(small),))],
         2_000_000,
     )
     halos = swap(faces)
-    masks = pltpu.VMEM((TILES, MODES, MODES, LANES), F32)
     r1, traces = call(
         local_rate,
-        (orders, g0, g1, vel, den, snd, g2, q0),
-        [SCALAR] * 3 + [LOCAL] * 5,
+        (coefs, g0, g1, q0),
+        [LOCAL, SCALAR, SCALAR, LOCAL],
         (bulk, jax.ShapeDtypeStruct((4,) + FACE, F32)),
         (LOCAL,) * 2,
-        [pltpu.VMEM(BULK, F32), masks],
+        [pltpu.VMEM(BULK, F32)],
         16_000_000,
     )
     faces = call(
         second_faces,
-        (orders, g0, g1, vel, den, snd, traces, *halos),
-        [SCALAR] * 3 + [LOCAL] * 8,
+        (coefs, g0, g1, traces, *halos),
+        [LOCAL, SCALAR, SCALAR] + [LOCAL] * 5,
         (face,) * 4,
         (LOCAL,) * 4,
         [pltpu.VMEM((4,) + plane, F32)],
@@ -475,19 +490,19 @@
     halo = pltpu.VMEM((2, 2) + FACE, F32)
     part = call(
         second_local,
-        (orders, g0, g1, vel, den, snd, g2, q0, r1, *halos),
-        [SCALAR] * 3 + [LOCAL] * 10,
+        (coefs, g0, g1, q0, r1, *halos),
+        [LOCAL, SCALAR, SCALAR] + [LOCAL] * 6,
         bulk,
         LOCAL,
-        [pltpu.VMEM(BULK, F32), pltpu.VMEM(BULK, F32), halo, masks],
+        [pltpu.VMEM(BULK, F32), pltpu.VMEM(BULK, F32), halo],
         20_000_000,
     )
     out = call(
         last_add,
-        (orders, g0, g1, part, *last),
-        [SCALAR] * 3 + [LOCAL] * 5,
+        (coefs, g0, g1, part, *last),
+        [LOCAL, SCALAR, SCALAR] + [LOCAL] * 5,
         jax.ShapeDtypeStruct(modal.shape, F32),
-        ANYWHERE,
+        FAR,
         [pltpu.VMEM(BULK, F32), halo, sems],
         4_000_000,
     )

time: 35.9 us -> 28.9 us (0.81)
  Pallas kernels: 17.2 us -> 12.7 us
  local copies, waits for them, and re-layouts: 4.46 us -> 0 us
  starting transfers between devices: 10.9 us -> 14.5 us
  waiting for transfers between devices: 1.68 us -> 0.1 us
    pallas_call x5, Pallas kernels: 17.2 us -> 12.7 us  [call(): pl.pallas_call(body, out_shape=outs, in_specs=specs, out_specs=out_specs,...]
    unnamed x14 -> x0, local copies, waits for them, and re-layouts: 4.46 us -> none
    ppermute x2, starting transfers between devices: 5.04 us -> 8.3 us  [exchange(): lax.ppermute(y_odd, 'grp', grp_perms[1])]
    ppermute x2, waiting for transfers between devices: 1.67 us -> 0.01 us  [exchange(): lax.ppermute(x_odd, both, dom_perms[1])]
  transfers between devices with their start and end apart: 8 -> 8, of which waited for: 1 -> 1; matrix products, arithmetic and copies ran while one was open for 0% -> 0% of each run, Pallas kernels for 35% -> 28%
where the time goes in v1:
time: 28.9 us; the launch traced here: 28.8 us
  starting transfers between devices  14.5 us (50%)
  Pallas kernels  12.7 us (44%)
  between operations  1.38 us (5%)
    pallas_call x5, Pallas kernels, call(): pl.pallas_call(body, out_shape=outs, in_specs=specs, out_specs=out_specs,...  12.7 us
    ppermute x2, starting transfers between devices, exchange(): lax.ppermute(y_odd, 'grp', grp_perms[1])  8.3 us
    ppermute x2, starting transfers between devices, exchange(): lax.ppermute(x_odd, both, dom_perms[1])  4.17 us
    ppermute x2, starting transfers between devices, exchange(): lax.ppermute(x_even, 'dom', dom_perms[0])  2.06 us
  transfers between devices with their start and end apart: 8, of which 1 were waited for; matrix products, arithmetic and copies ran while one was open for 0% of the time, Pallas kernels for 28%

profile of v1, /device:TPU:24, one launch (start us, length us, event | category | flops | bytes accessed | tf_op | source)
XLA Modules:
  0.0 28.8 jit_solution(108867469723624426)
XLA Ops:
  0.0 2.1 %first_faces.1 = (f32[2,5,8,64,128]{4,3,2,1,0:T(8,128)S(1)}, f32[2,17,8,128]{3,2,1,0:T(8,128)S(1)}, f32[2,5,64,128]{3,2,1,0:T(8,128)S(1)}, f32[2,5,64,128]{3,2,1...) custom-call(f32[3,256]{1,0:T(4,128)} %refs_0_.1, f32[256]{0:T(256)} %refs_1_.1, ...), custom_call_target="tpu_custom_call" | custom-call | flops 2000000 | bytes 2600000 | tf_op jit(solution)/shard_map/first_faces/pallas_call | solution.py:411
  2.1 1.6 %collective-permute-start = (f32[2,5,64,128]{3,2,1,0:T(8,128)S(1)}, f32[2,5,64,128]{3,2,1,0:T(8,128)S(1)}, u32[]{:S(2)}, u32[]{:S(2)}) collective-permute-start(f32[2,5,64,128]{3,2,1,0:T(8,128)S(1)} %get-tuple-element.20), channel_id=1, source_target_pairs={{0,8},{8,0},{16,24},{24,16},{32,40},{40,32},{48,56},{56,48},{64,72... | collective-permute-start | bytes 983048 | tf_op jit(solution)/shard_map/ppermute | solution.py:427
  3.7 2.3 %collective-permute-start.1 = (f32[2,5,64,128]{3,2,1,0:T(8,128)S(1)}, f32[2,5,64,128]{3,2,1,0:T(8,128)S(1)}, u32[]{:S(2)}, u32[]{:S(2)}) collective-permute-start(f32[2,5,64,128]{3,2,1,0:T(8,128)S(1)} %get-tuple-element.21), channel_id=1, source_target_pairs={{0,1},{1,0},{2,3},{3,2},{4,5},{5,4},{6,7},{7,6},{8,16},{9,17},{10,... | collective-permute-start | bytes 983048 | tf_op jit(solution)/shard_map/ppermute | solution.py:428
  6.0 0.0 collective-permute-start.2
  6.0 4.1 %collective-permute-start.3 = (f32[2,5,64,128]{3,2,1,0:T(8,128)S(1)}, f32[2,5,64,128]{3,2,1,0:T(8,128)S(1)}, u32[]{:S(2)}, u32[]{:S(2)}) collective-permute-start(f32[2,5,64,128]{3,2,1,0:T(8,128)S(1)} %get-tuple-element.23), channel_id=1, source_target_pairs={{0,7},{1,2},{2,1},{3,4},{4,3},{5,6},{6,5},{7,0},{8,15},{9,10},{10,... | collective-permute-start | bytes 983048 | tf_op jit(solution)/shard_map/ppermute | solution.py:430
  11.4 3.6 %local_rate.1 = (f32[2,5,8,64,128]{4,3,2,1,0:T(8,128)S(1)}, f32[4,2,5,64,128]{4,3,2,1,0:T(8,128)S(1)}) custom-call(f32[2,17,8,128]{3,2,1,0:T(8,128)S(1)} %get-tuple-element.17.coefs, f32[1]{0:T(128)S(6)} %copy.9.g0, f32[1]{0:T(128)S(6)} %copy.10.g1, f32[2,5,8,64,128]{4,3,2,1,0:T(8,128)S(1)} %get-tuple-element.18.q0), custom_call_target="tpu_custom_call" | custom-call | flops 16000000 | bytes 2600000 | tf_op jit(solution)/shard_map/local_rate/pallas_call | solution.py:411
  15.0 0.0 collective-permute-done.xe
  15.0 0.0 collective-permute-done.1.xo
  15.0 0.0 collective-permute-done.2.ye
  15.0 0.0 collective-permute-done.3.yo
  15.0 0.6 %second_faces.1 = (f32[2,5,64,128]{3,2,1,0:T(8,128)S(1)}, f32[2,5,64,128]{3,2,1,0:T(8,128)S(1)}, f32[2,5,64,128]{3,2,1,0:T(8,128)S(1)}, f32[2,5,64,128]{3,2,1,0:T(8,128)S(1)}) custom-call(f32[2,17,8,128]{3,2,1,0:T(8,128)S(1)} %get-tuple-element.17.coefs, f32[1]{0:T(128)S(6)} %copy.9.g0, f32[1]{0:T(128)S(6)} %copy.10.g1, ...), custom_call_target="tpu_custom_call" | custom-call | flops 2000000 | bytes 2600000 | tf_op jit(solution)/shard_map/second_faces/pallas_call | solution.py:411
  15.6 0.5 %collective-permute-start.4 = (f32[2,5,64,128]{3,2,1,0:T(8,128)S(1)}, f32[2,5,64,128]{3,2,1,0:T(8,128)S(1)}, u32[]{:S(2)}, u32[]{:S(2)}) collective-permute-start(f32[2,5,64,128]{3,2,1,0:T(8,128)S(1)} %get-tuple-element.25), channel_id=1, source_target_pairs={{0,8},{8,0},{16,24},{24,16},{32,40},{40,32},{48,56},{56,48},{64,72... | collective-permute-start | bytes 983048 | tf_op jit(solution)/shard_map/ppermute | solution.py:427
  16.1 1.9 %collective-permute-start.5 = (f32[2,5,64,128]{3,2,1,0:T(8,128)S(1)}, f32[2,5,64,128]{3,2,1,0:T(8,128)S(1)}, u32[]{:S(2)}, u32[]{:S(2)}) collective-permute-start(f32[2,5,64,128]{3,2,1,0:T(8,128)S(1)} %get-tuple-element.26), channel_id=1, source_target_pairs={{0,1},{1,0},{2,3},{3,2},{4,5},{5,4},{6,7},{7,6},{8,16},{9,17},{10,... | collective-permute-start | bytes 983048 | tf_op jit(solution)/shard_map/ppermute | solution.py:428
  18.0 0.0 collective-permute-start.6
  18.0 4.2 %collective-permute-start.7 = (f32[2,5,64,128]{3,2,1,0:T(8,128)S(1)}, f32[2,5,64,128]{3,2,1,0:T(8,128)S(1)}, u32[]{:S(2)}, u32[]{:S(2)}) collective-permute-start(f32[2,5,64,128]{3,2,1,0:T(8,128)S(1)} %get-tuple-element.28), channel_id=1, source_target_pairs={{0,7},{1,2},{2,1},{3,4},{4,3},{5,6},{6,5},{7,0},{8,15},{9,10},{10,... | collective-permute-start | bytes 983048 | tf_op jit(solution)/shard_map/ppermute | solution.py:430
  22.2 4.6 %second_local.1.part = f32[2,5,8,64,128]{4,3,2,1,0:T(8,128)S(1)} custom-call(f32[2,17,8,128]{3,2,1,0:T(8,128)S(1)} %get-tuple-element.17.coefs, f32[1]{0:T(128)S(6)} %copy.9.g0, f32[1]{0:T(128)S(6)} %copy.10.g1, f32[2,5,8,64,128]{4,3,2,1,0:T(8,128)S(1)} %get-tuple-element.18.q0, f32[2,5,8,64,128]{4,3,2,1,0:T(8,128)S(1)} %get-tuple-element.19.r1, ...), custom_call_target="tpu_custom_call" | custom-call | flops 20000000 | bytes 2600000 | tf_op jit(solution)/shard_map/second_local/pallas_call | solution.py:411
  26.8 0.0 collective-permute-done.4.xe
  26.8 0.0 collective-permute-done.5.xo
  26.8 0.0 collective-permute-done.6.ye
  26.9 0.1 collective-permute-done.7.yo
  26.9 1.8 %last_add.1 = f32[5,8,64,256]{3,2,1,0:T(8,128)} custom-call(f32[2,17,8,128]{3,2,1,0:T(8,128)S(1)} %get-tuple-element.17.coefs, f32[1]{0:T(128)S(6)} %copy.9.g0, f32[1]{0:T(128)S(6)} %copy.10.g1, f32[2,5,8,64,128]{4,3,2,1,0:T(8,128)S(1)} %second_local.1.part, f32[2,5,64,128]{3,2,1,0:T(8,128)S(1)} %collective-permute-done.4.xe, ...), custom_call_target="tpu_custom_call" | custom-call | flops 4000000 | bytes 2600000 | tf_op jit(solution)/shard_map/last_add/pallas_call | solution.py:411
Async XLA Ops:
  2.1 12.9 %collective-permute-start = (f32[2,5,64,128]{3,2,1,0:T(8,128)S(1)}, f32[2,5,64,128]{3,2,1,0:T(8,128)S(1)}, u32[]{:S(2)}, u32[]{:S(2)}) collective-permute-start(f32[2,5,64,128]{3,2,1,0:T(8,128)S(1)} %get-tuple-element.20), channel_id=1, source_target_pairs={{0,8},{8,0},{16,24},{24,16},{32,40},{40,32},{48,56},{56,48},{64,72... | collective-permute-start | bytes 983048 | tf_op jit(solution)/shard_map/ppermute | solution.py:427
  3.7 11.3 %collective-permute-start.1 = (f32[2,5,64,128]{3,2,1,0:T(8,128)S(1)}, f32[2,5,64,128]{3,2,1,0:T(8,128)S(1)}, u32[]{:S(2)}, u32[]{:S(2)}) collective-permute-start(f32[2,5,64,128]{3,2,1,0:T(8,128)S(1)} %get-tuple-element.21), channel_id=1, source_target_pairs={{0,1},{1,0},{2,3},{3,2},{4,5},{5,4},{6,7},{7,6},{8,16},{9,17},{10,... | collective-permute-start | bytes 983048 | tf_op jit(solution)/shard_map/ppermute | solution.py:428
  6.0 9.0 %collective-permute-start.2 = (f32[2,5,64,128]{3,2,1,0:T(8,128)S(1)}, f32[2,5,64,128]{3,2,1,0:T(8,128)S(1)}, u32[]{:S(2)}, u32[]{:S(2)}) collective-permute-start(f32[2,5,64,128]{3,2,1,0:T(8,128)S(1)} %get-tuple-element.22), channel_id=1, source_target_pairs={{0,1},{1,0},{2,3},{3,2},{4,5},{5,4},{6,7},{7,6},{8,9},{9,8},{10,11... | collective-permute-start | bytes 983048 | tf_op jit(solution)/shard_map/ppermute | solution.py:429
  6.0 9.0 %collective-permute-start.3 = (f32[2,5,64,128]{3,2,1,0:T(8,128)S(1)}, f32[2,5,64,128]{3,2,1,0:T(8,128)S(1)}, u32[]{:S(2)}, u32[]{:S(2)}) collective-permute-start(f32[2,5,64,128]{3,2,1,0:T(8,128)S(1)} %get-tuple-element.23), channel_id=1, source_target_pairs={{0,7},{1,2},{2,1},{3,4},{4,3},{5,6},{6,5},{7,0},{8,15},{9,10},{10,... | collective-permute-start | bytes 983048 | tf_op jit(solution)/shard_map/ppermute | solution.py:430
  15.6 11.2 %collective-permute-start.4 = (f32[2,5,64,128]{3,2,1,0:T(8,128)S(1)}, f32[2,5,64,128]{3,2,1,0:T(8,128)S(1)}, u32[]{:S(2)}, u32[]{:S(2)}) collective-permute-start(f32[2,5,64,128]{3,2,1,0:T(8,128)S(1)} %get-tuple-element.25), channel_id=1, source_target_pairs={{0,8},{8,0},{16,24},{24,16},{32,40},{40,32},{48,56},{56,48},{64,72... | collective-permute-start | bytes 983048 | tf_op jit(solution)/shard_map/ppermute | solution.py:427
  16.1 10.7 %collective-permute-start.5 = (f32[2,5,64,128]{3,2,1,0:T(8,128)S(1)}, f32[2,5,64,128]{3,2,1,0:T(8,128)S(1)}, u32[]{:S(2)}, u32[]{:S(2)}) collective-permute-start(f32[2,5,64,128]{3,2,1,0:T(8,128)S(1)} %get-tuple-element.26), channel_id=1, source_target_pairs={{0,1},{1,0},{2,3},{3,2},{4,5},{5,4},{6,7},{7,6},{8,16},{9,17},{10,... | collective-permute-start | bytes 983048 | tf_op jit(solution)/shard_map/ppermute | solution.py:428
  18.0 8.8 %collective-permute-start.6 = (f32[2,5,64,128]{3,2,1,0:T(8,128)S(1)}, f32[2,5,64,128]{3,2,1,0:T(8,128)S(1)}, u32[]{:S(2)}, u32[]{:S(2)}) collective-permute-start(f32[2,5,64,128]{3,2,1,0:T(8,128)S(1)} %get-tuple-element.27), channel_id=1, source_target_pairs={{0,1},{1,0},{2,3},{3,2},{4,5},{5,4},{6,7},{7,6},{8,9},{9,8},{10,11... | collective-permute-start | bytes 983048 | tf_op jit(solution)/shard_map/ppermute | solution.py:429
  18.0 8.9 %collective-permute-start.7 = (f32[2,5,64,128]{3,2,1,0:T(8,128)S(1)}, f32[2,5,64,128]{3,2,1,0:T(8,128)S(1)}, u32[]{:S(2)}, u32[]{:S(2)}) collective-permute-start(f32[2,5,64,128]{3,2,1,0:T(8,128)S(1)} %get-tuple-element.28), channel_id=1, source_target_pairs={{0,7},{1,2},{2,1},{3,4},{4,3},{5,6},{6,5},{7,0},{8,15},{9,10},{10,... | collective-permute-start | bytes 983048 | tf_op jit(solution)/shard_map/ppermute | solution.py:430

commit v2 on v1

--- a/solution.py
+++ b/solution.py
@@ -39,8 +39,8 @@
     return out
 
 
-FLOW, RHO, INVERSE, STIFF, THIRD, LEVEL, WEIGHT = 0, 3, 4, 5, 6, 7, 15
-COEFS = (TILES, 17, MODES, LANES)
+FLOW, RHO, INVERSE, STIFF, THIRD, LEVEL, WEIGHT, LIVE = 0, 3, 4, 5, 6, 7, 15, 17
+COEFS = (TILES, 25, MODES, LANES)
 
 
 def spread(ref, t, row=0):
@@ -62,6 +62,7 @@
         order = jnp.broadcast_to(orders[pl.ds(t, 1)].reshape(1, 1), (MODES, LANES))
         for k in range(MODES):
             coefs[t, LEVEL + k] = jnp.where(jnp.maximum(third, k) <= order, 1.0, 0.0).astype(F32)
+            coefs[t, LIVE + k] = jnp.where(order >= k, 1.0, 0.0).astype(F32)
         for parity in range(2):
             coefs[t, WEIGHT + parity] = sum(
                 jnp.where(order >= m, m + 0.5, 0.0).astype(F32) for m in range(parity, MODES, 2)
@@ -83,15 +84,16 @@
     return out
 
 
-def write_faces(d, sign, coef, even_of, odd_of, slots, t):
+def write_faces(d, sign, coef, sums, slots, t):
     us, rho, inv, stiff = coef
     half = 0.5 * sign
     u = half * us[d]
     near, far = HALF_WAVE + u, HALF_WAVE - u
     rho, inv, stiff = half * rho, half * inv, half * stiff
+
     for m in range(MODES):
-        even, odd = even_of(m), odd_of(m)
-        odd = [sign * a for a in odd]
+        even = [sums[2 * d, f, rows(m), :] for f in range(FIELDS)]
+        odd = [sign * sums[2 * d + 1, f, rows(m), :] for f in range(FIELDS)]
         one = flux([a + b for a, b in zip(even, odd)], d, near, rho, inv, stiff)
         two = flux([a - b for a, b in zip(even, odd)], d, far, -rho, -inv, -stiff)
         for f in range(FIELDS):
@@ -110,20 +112,20 @@
     loads = [pltpu.make_async_copy(a, b, small_sems.at[i]) for i, (a, b) in enumerate(zip(small, held))]
     for load in loads:
         load.start()
-    copies = {}
-    for t in range(TILES):
-        for f in range(FIELDS):
-            copies[t, f] = pltpu.make_async_copy(
-                modal.at[f, :, :, pl.ds(t * LANES, LANES)], q0.at[t, f], sems.at[t, f]
-            )
-            copies[t, f].start()
+    def copy(t, f):
+        return pltpu.make_async_copy(modal.at[f, :, :, pl.ds(t * LANES, LANES)], q0.at[t, f], sems.at[t, f])
+
+    for t in range(TILES):
+        for f in range(FIELDS):
+            copy(t, f).start()
     (sign_x, _), (sign_y, _) = place()
     for load in loads:
         load.wait()
     store_coefs(coefs, *held)
-    for t in range(TILES):
-        for f in range(FIELDS):
-            copies[t, f].wait()
+
+    for t in range(TILES):
+        for f in range(FIELDS):
+            copy(t, f).wait()
             e0 = [None] * MODES
             o0 = [None] * MODES
             for a in range(MODES):
@@ -146,15 +148,7 @@
                 sums[1, f, rows(b), :] = o0[b]
         coef = medium(coefs, t)
         for d, sign, slots in ((0, sign_x, (x_even, x_odd)), (1, sign_y, (y_even, y_odd))):
-            write_faces(
-                d,
-                sign,
-                coef,
-                lambda m: [sums[2 * d, f, rows(m), :] for f in range(FIELDS)],
-                lambda m: [sums[2 * d + 1, f, rows(m), :] for f in range(FIELDS)],
-                slots,
-                t,
-            )
+            write_faces(d, sign, coef, sums, slots, t)
 
 
 def scaled(coef, d, s):
@@ -296,43 +290,40 @@
     first_direction(q0, acc, coefs, metric, TIME_STEP, finish)
 
 
-def second_faces(coefs, g0, g1, traces, xe, xo, ye, yo, x_even, x_odd, y_even, y_odd, face):
+def second_faces(coefs, g0, g1, traces, xo, xe, yo, ye, x_even, x_odd, y_even, y_odd, sums):
     metric = g0[0], g1[0]
     (sign_x, has_x), (sign_y, has_y) = place()
+    sides = ((0, (xe, xo), sign_x, has_x), (1, (ye, yo), sign_y, has_y))
+
     for t in range(TILES):
         mask = [coefs[t, LEVEL + k] for k in range(MODES)]
         weights = [coefs[t, WEIGHT + parity] for parity in range(2)]
         scale = [SECTION_B1 * TIME_STEP * metric[d] for d in range(2)]
+
         for f in range(FIELDS):
             pairs = []
             across = []
-            for d, slots, sign, has in ((0, (xe, xo), sign_x, has_x), (1, (ye, yo), sign_y, has_y)):
-                pair = [halo_pair(slots, sign, has, t, f, m, scale[d]) for m in range(MODES)]
+            for d, slots, sign, has in sides:
+                pair = [
+                    [mask[m] * x for x in halo_pair(slots, sign, has, t, f, m, scale[d])] for m in range(MODES)
+                ]
                 pairs.append(pair)
                 across.append(
                     [
-                        [sum(mask[m] * pair[m][kind] for m in range(parity, MODES, 2)) for parity in range(2)]
+                        [sum(pair[m][kind] for m in range(parity + 2, MODES, 2)) + pair[parity][kind] for parity in range(2)]
                         for kind in range(2)
                     ]
                 )
             for d in range(2):
                 for m in range(MODES):
+                    heavy = (m + 0.5) * mask[m]
                     for parity in range(2):
-                        add = weights[parity] * pairs[d][m][parity] + (m + 0.5) * across[1 - d][m % 2][parity]
-                        face[2 * d + parity, f, rows(m), :] = (
-                            traces[2 * d + parity, t, f, rows(m), :] + mask[m] * add
+                        sums[2 * d + parity, f, rows(m), :] = traces[2 * d + parity, t, f, rows(m), :] + (
+                            weights[parity] * pairs[d][m][parity] + heavy * across[1 - d][m % 2][parity]
                         )
         coef = medium(coefs, t)
         for d, sign, slots in ((0, sign_x, (x_even, x_odd)), (1, sign_y, (y_even, y_odd))):
-            write_faces(
-                d,
-                sign,
-                coef,
-                lambda m: [face[2 * d, f, rows(m), :] for f in range(FIELDS)],
-                lambda m: [face[2 * d + 1, f, rows(m), :] for f in range(FIELDS)],
-                slots,
-                t,
-            )
+            write_faces(d, sign, coef, sums, slots, t)
 
 
 def store_halos(halo, xe, xo, ye, yo, metric, s):
@@ -355,7 +346,7 @@
     return (a + 0.5) * halo[0, a % 2, t, f, rows(b), :] + weight * halo[1, kind, t, f, rows(a), :]
 
 
-def second_local(coefs, g0, g1, q0, r1, xe, xo, ye, yo, part, q1, acc, halo):
+def second_local(coefs, g0, g1, q0, r1, xo, xe, yo, ye, part, q1, acc, halo):
     metric = g0[0], g1[0]
     store_halos(halo, xe, xo, ye, yo, metric, TIME_STEP)
     for t in range(TILES):
@@ -384,22 +375,40 @@
     first_direction(q1, acc, coefs, metric, SECTION_B2 * TIME_STEP, finish)
 
 
-def last_add(coefs, g0, g1, part, xe, xo, ye, yo, out, done, halo, sems):
+def last_add(coefs, g0, g1, part, xo, xe, yo, ye, out, done, sems):
     metric = g0[0], g1[0]
-    store_halos(halo, xe, xo, ye, yo, metric, SECTION_B2 * TIME_STEP)
-    copies = []
-    for t in range(TILES):
+    (sign_x, has_x), (sign_y, has_y) = place()
+    sides = ((0, (xe, xo), sign_x, has_x), (1, (ye, yo), sign_y, has_y))
+
+    def copy(t, f):
+        lanes = pl.ds(pl.multiple_of(t * LANES, LANES), LANES)
+        return pltpu.make_async_copy(done.at[t, f], out.at[f, :, :, lanes], sems.at[t, f])
+
+    def tile(t, carry):
         mask = [coefs[t, LEVEL + k] for k in range(MODES)]
-        for f in range(FIELDS):
+        weight = [(m + 0.5) * coefs[t, LIVE + m] for m in range(MODES)]
+
+        def field(f, carry):
+            first, second = (
+                [
+                    [mask[m] * x for x in halo_pair(slots, sign, has, t, f, m, SECTION_B2 * TIME_STEP * metric[d])]
+                    for m in range(MODES)
+                ]
+                for d, slots, sign, has in sides
+            )
             for a in range(MODES):
                 for b in range(MODES):
-                    term = halo_term(halo, t, f, a, b, b + 0.5, b % 2)
-                    done[t, f, a, rows(b), :] = part[t, f, a, rows(b), :] + mask[max(a, b)] * term
-            copy = pltpu.make_async_copy(done.at[t, f], out.at[f, :, :, pl.ds(t * LANES, LANES)], sems.at[t, f])
-            copy.start()
-            copies.append(copy)
-    for copy in copies:
-        copy.wait()
+                    term = weight[a] * first[b][a % 2] + weight[b] * second[a][b % 2]
+                    done[t, f, a, rows(b), :] = part[t, f, a, rows(b), :] + term
+            copy(t, f).start()
+            return carry
+
+        return lax.fori_loop(0, FIELDS, field, carry)
+
+    lax.fori_loop(0, TILES, tile, 0)
+    for t in range(TILES):
+        for f in range(FIELDS):
+            copy(t, f).wait()
 
 
 SCALAR = pl.BlockSpec(memory_space=pltpu.SMEM)
@@ -424,10 +433,10 @@
     x_even, x_odd, y_even, y_odd = faces
     both = ("dom", "grp")
     return (
+        lax.ppermute(x_odd, both, dom_perms[1]),
         lax.ppermute(x_even, "dom", dom_perms[0]),
-        lax.ppermute(x_odd, both, dom_perms[1]),
+        lax.ppermute(y_odd, "grp", grp_perms[1]),
         lax.ppermute(y_even, "grp", grp_perms[0]),
-        lax.ppermute(y_odd, "grp", grp_perms[1]),
     )
 
 
@@ -503,7 +512,7 @@
         [LOCAL, SCALAR, SCALAR] + [LOCAL] * 5,
         jax.ShapeDtypeStruct(modal.shape, F32),
         FAR,
-        [pltpu.VMEM(BULK, F32), halo, sems],
+        [pltpu.VMEM(BULK, F32), sems],
         4_000_000,
     )
     return out.reshape(shape)

time: 28.9 us -> 28 us (0.969)
  starting transfers between devices: 14.5 us -> 11 us
  waiting for transfers between devices: 0.1 us -> 3.06 us
  Pallas kernels: 12.7 us -> 12.4 us
    ppermute x2, starting transfers between devices: 8.3 us -> 5.48 us  [exchange(): lax.ppermute(y_odd, 'grp', grp_perms[1])]
    ppermute x2, waiting for transfers between devices: 0.01 us -> 2.5 us  [exchange(): lax.ppermute(x_odd, both, dom_perms[1])]
    ppermute x2, starting transfers between devices: 2.06 us -> 0.05 us  [exchange(): lax.ppermute(x_even, 'dom', dom_perms[0])]
    ppermute x2, starting transfers between devices: 4.17 us -> 5.5 us  [exchange(): lax.ppermute(x_odd, both, dom_perms[1])]
    ppermute x2, waiting for transfers between devices: 0.01 us -> 0.55 us  [exchange(): lax.ppermute(x_even, 'dom', dom_perms[0])]
    pallas_call x5, Pallas kernels: 12.7 us -> 12.4 us  [call(): pl.pallas_call(body, out_shape=outs, in_specs=specs, out_specs=out_specs,...]
  transfers between devices with their start and end apart: 8 -> 8, of which waited for: 1 -> 3; matrix products, arithmetic and copies ran while one was open for 0% -> 0% of each run, Pallas kernels for 28% -> 29%
where the time goes in v2:
time: 28 us; the launch traced here: 27.8 us
  Pallas kernels  12.4 us (44%)
  starting transfers between devices  11 us (39%)
  waiting for transfers between devices  3.06 us (11%)
  between operations  1.34 us (5%)
    pallas_call x5, Pallas kernels, call(): pl.pallas_call(body, out_shape=outs, in_specs=specs, out_specs=out_specs,...  12.4 us
    ppermute x2, starting transfers between devices, exchange(): lax.ppermute(x_odd, both, dom_perms[1])  5.5 us
    ppermute x2, starting transfers between devices, exchange(): lax.ppermute(y_odd, 'grp', grp_perms[1])  5.48 us
    ppermute x2, waiting for transfers between devices, exchange(): lax.ppermute(x_odd, both, dom_perms[1])  2.5 us
  transfers between devices with their start and end apart: 8, of which 3 were waited for; matrix products, arithmetic and copies ran while one was open for 0% of the time, Pallas kernels for 29%

profile of v2, /device:TPU:24, one launch (start us, length us, event | category | flops | bytes accessed | tf_op | source)
XLA Modules:
  0.0 27.8 jit_solution(2190343920499673734)
XLA Ops:
  0.0 2.1 %first_faces.1 = (f32[2,5,8,64,128]{4,3,2,1,0:T(8,128)S(1)}, f32[2,25,8,128]{3,2,1,0:T(8,128)S(1)}, f32[2,5,64,128]{3,2,1,0:T(8,128)S(1)}, f32[2,5,64,128]{3,2,1...) custom-call(f32[3,256]{1,0:T(4,128)} %refs_0_.1, f32[256]{0:T(256)} %refs_1_.1, ...), custom_call_target="tpu_custom_call" | custom-call | flops 2000000 | bytes 2600000 | tf_op jit(solution)/shard_map/first_faces/pallas_call | solution.py:420
  2.1 3.0 %collective-permute-start = (f32[2,5,64,128]{3,2,1,0:T(8,128)S(1)}, f32[2,5,64,128]{3,2,1,0:T(8,128)S(1)}, u32[]{:S(2)}, u32[]{:S(2)}) collective-permute-start(f32[2,5,64,128]{3,2,1,0:T(8,128)S(1)} %get-tuple-element.20), channel_id=1, source_target_pairs={{0,1},{1,0},{2,3},{3,2},{4,5},{5,4},{6,7},{7,6},{8,16},{9,17},{10,... | collective-permute-start | bytes 983048 | tf_op jit(solution)/shard_map/ppermute | solution.py:436
  5.1 0.0 collective-permute-start.1
  5.2 3.2 %collective-permute-start.2 = (f32[2,5,64,128]{3,2,1,0:T(8,128)S(1)}, f32[2,5,64,128]{3,2,1,0:T(8,128)S(1)}, u32[]{:S(2)}, u32[]{:S(2)}) collective-permute-start(f32[2,5,64,128]{3,2,1,0:T(8,128)S(1)} %get-tuple-element.22), channel_id=1, source_target_pairs={{0,7},{1,2},{2,1},{3,4},{4,3},{5,6},{6,5},{7,0},{8,15},{9,10},{10,... | collective-permute-start | bytes 983048 | tf_op jit(solution)/shard_map/ppermute | solution.py:438
  8.3 0.0 collective-permute-start.3
  9.7 3.6 %local_rate.1 = (f32[2,5,8,64,128]{4,3,2,1,0:T(8,128)S(1)}, f32[4,2,5,64,128]{4,3,2,1,0:T(8,128)S(1)}) custom-call(f32[2,25,8,128]{3,2,1,0:T(8,128)S(1)} %get-tuple-element.17.coefs, f32[1]{0:T(128)S(6)} %copy.9.g0, f32[1]{0:T(128)S(6)} %copy.10.g1, f32[2,5,8,64,128]{4,3,2,1,0:T(8,128)S(1)} %get-tuple-element.18.q0), custom_call_target="tpu_custom_call" | custom-call | flops 16000000 | bytes 2600000 | tf_op jit(solution)/shard_map/local_rate/pallas_call | solution.py:420
  13.2 0.6 %collective-permute-done.xo = f32[2,5,64,128]{3,2,1,0:T(8,128)S(1)} collective-permute-done((f32[2,5,64,128]{3,2,1,0:T(8,128)S(1)}, f32[2,5,64,128]{3,2,1,0:T(8,128)S(1)}, u32[]{:S(2)}, u32[]{:S(2)}) %collective-permute-start) | collective-permute-done | bytes 327712 | tf_op jit(solution)/shard_map/ppermute | solution.py:436
  13.8 0.5 %collective-permute-done.1.xe = f32[2,5,64,128]{3,2,1,0:T(8,128)S(1)} collective-permute-done((f32[2,5,64,128]{3,2,1,0:T(8,128)S(1)}, f32[2,5,64,128]{3,2,1,0:T(8,128)S(1)}, u32[]{:S(2)}, u32[]{:S(2)}) %collective-permute-start.1) | collective-permute-done | bytes 327712 | tf_op jit(solution)/shard_map/ppermute | solution.py:437
  14.3 0.0 collective-permute-done.2.yo
  14.3 0.0 collective-permute-done.3.ye
  14.3 0.6 %second_faces.1 = (f32[2,5,64,128]{3,2,1,0:T(8,128)S(1)}, f32[2,5,64,128]{3,2,1,0:T(8,128)S(1)}, f32[2,5,64,128]{3,2,1,0:T(8,128)S(1)}, f32[2,5,64,128]{3,2,1,0:T(8,128)S(1)}) custom-call(f32[2,25,8,128]{3,2,1,0:T(8,128)S(1)} %get-tuple-element.17.coefs, f32[1]{0:T(128)S(6)} %copy.9.g0, f32[1]{0:T(128)S(6)} %copy.10.g1, ...), custom_call_target="tpu_custom_call" | custom-call | flops 2000000 | bytes 2600000 | tf_op jit(solution)/shard_map/second_faces/pallas_call | solution.py:420
  14.9 2.5 %collective-permute-start.4 = (f32[2,5,64,128]{3,2,1,0:T(8,128)S(1)}, f32[2,5,64,128]{3,2,1,0:T(8,128)S(1)}, u32[]{:S(2)}, u32[]{:S(2)}) collective-permute-start(f32[2,5,64,128]{3,2,1,0:T(8,128)S(1)} %get-tuple-element.25), channel_id=1, source_target_pairs={{0,1},{1,0},{2,3},{3,2},{4,5},{5,4},{6,7},{7,6},{8,16},{9,17},{10,... | collective-permute-start | bytes 983048 | tf_op jit(solution)/shard_map/ppermute | solution.py:436
  17.4 0.0 collective-permute-start.5
  17.4 2.3 %collective-permute-start.6 = (f32[2,5,64,128]{3,2,1,0:T(8,128)S(1)}, f32[2,5,64,128]{3,2,1,0:T(8,128)S(1)}, u32[]{:S(2)}, u32[]{:S(2)}) collective-permute-start(f32[2,5,64,128]{3,2,1,0:T(8,128)S(1)} %get-tuple-element.27), channel_id=1, source_target_pairs={{0,7},{1,2},{2,1},{3,4},{4,3},{5,6},{6,5},{7,0},{8,15},{9,10},{10,... | collective-permute-start | bytes 983048 | tf_op jit(solution)/shard_map/ppermute | solution.py:438
  19.7 0.0 collective-permute-start.7
  19.7 4.5 %second_local.1.part = f32[2,5,8,64,128]{4,3,2,1,0:T(8,128)S(1)} custom-call(f32[2,25,8,128]{3,2,1,0:T(8,128)S(1)} %get-tuple-element.17.coefs, f32[1]{0:T(128)S(6)} %copy.9.g0, f32[1]{0:T(128)S(6)} %copy.10.g1, f32[2,5,8,64,128]{4,3,2,1,0:T(8,128)S(1)} %get-tuple-element.18.q0, f32[2,5,8,64,128]{4,3,2,1,0:T(8,128)S(1)} %get-tuple-element.19.r1, ...), custom_call_target="tpu_custom_call" | custom-call | flops 20000000 | bytes 2600000 | tf_op jit(solution)/shard_map/second_local/pallas_call | solution.py:420
  24.2 1.9 %collective-permute-done.4.xo = f32[2,5,64,128]{3,2,1,0:T(8,128)S(1)} collective-permute-done((f32[2,5,64,128]{3,2,1,0:T(8,128)S(1)}, f32[2,5,64,128]{3,2,1,0:T(8,128)S(1)}, u32[]{:S(2)}, u32[]{:S(2)}) %collective-permute-start.4) | collective-permute-done | bytes 327712 | tf_op jit(solution)/shard_map/ppermute | solution.py:436
  26.2 0.0 collective-permute-done.5.xe
  26.2 0.0 collective-permute-done.6.yo
  26.2 0.0 collective-permute-done.7.ye
  26.2 1.7 %last_add.1 = f32[5,8,64,256]{3,2,1,0:T(8,128)} custom-call(f32[2,25,8,128]{3,2,1,0:T(8,128)S(1)} %get-tuple-element.17.coefs, f32[1]{0:T(128)S(6)} %copy.9.g0, f32[1]{0:T(128)S(6)} %copy.10.g1, f32[2,5,8,64,128]{4,3,2,1,0:T(8,128)S(1)} %second_local.1.part, f32[2,5,64,128]{3,2,1,0:T(8,128)S(1)} %collective-permute-done.4.xo, ...), custom_call_target="tpu_custom_call" | custom-call | flops 4000000 | bytes 2600000 | tf_op jit(solution)/shard_map/last_add/pallas_call | solution.py:420
Async XLA Ops:
  2.1 11.6 %collective-permute-start = (f32[2,5,64,128]{3,2,1,0:T(8,128)S(1)}, f32[2,5,64,128]{3,2,1,0:T(8,128)S(1)}, u32[]{:S(2)}, u32[]{:S(2)}) collective-permute-start(f32[2,5,64,128]{3,2,1,0:T(8,128)S(1)} %get-tuple-element.20), channel_id=1, source_target_pairs={{0,1},{1,0},{2,3},{3,2},{4,5},{5,4},{6,7},{7,6},{8,16},{9,17},{10,... | collective-permute-start | bytes 983048 | tf_op jit(solution)/shard_map/ppermute | solution.py:436
  5.1 9.2 %collective-permute-start.1 = (f32[2,5,64,128]{3,2,1,0:T(8,128)S(1)}, f32[2,5,64,128]{3,2,1,0:T(8,128)S(1)}, u32[]{:S(2)}, u32[]{:S(2)}) collective-permute-start(f32[2,5,64,128]{3,2,1,0:T(8,128)S(1)} %get-tuple-element.21), channel_id=1, source_target_pairs={{0,8},{8,0},{16,24},{24,16},{32,40},{40,32},{48,56},{56,48},{64,72... | collective-permute-start | bytes 983048 | tf_op jit(solution)/shard_map/ppermute | solution.py:437
  5.2 9.1 %collective-permute-start.2 = (f32[2,5,64,128]{3,2,1,0:T(8,128)S(1)}, f32[2,5,64,128]{3,2,1,0:T(8,128)S(1)}, u32[]{:S(2)}, u32[]{:S(2)}) collective-permute-start(f32[2,5,64,128]{3,2,1,0:T(8,128)S(1)} %get-tuple-element.22), channel_id=1, source_target_pairs={{0,7},{1,2},{2,1},{3,4},{4,3},{5,6},{6,5},{7,0},{8,15},{9,10},{10,... | collective-permute-start | bytes 983048 | tf_op jit(solution)/shard_map/ppermute | solution.py:438
  8.3 6.0 %collective-permute-start.3 = (f32[2,5,64,128]{3,2,1,0:T(8,128)S(1)}, f32[2,5,64,128]{3,2,1,0:T(8,128)S(1)}, u32[]{:S(2)}, u32[]{:S(2)}) collective-permute-start(f32[2,5,64,128]{3,2,1,0:T(8,128)S(1)} %get-tuple-element.23), channel_id=1, source_target_pairs={{0,1},{1,0},{2,3},{3,2},{4,5},{5,4},{6,7},{7,6},{8,9},{9,8},{10,11... | collective-permute-start | bytes 983048 | tf_op jit(solution)/shard_map/ppermute | solution.py:439
  14.9 11.2 %collective-permute-start.4 = (f32[2,5,64,128]{3,2,1,0:T(8,128)S(1)}, f32[2,5,64,128]{3,2,1,0:T(8,128)S(1)}, u32[]{:S(2)}, u32[]{:S(2)}) collective-permute-start(f32[2,5,64,128]{3,2,1,0:T(8,128)S(1)} %get-tuple-element.25), channel_id=1, source_target_pairs={{0,1},{1,0},{2,3},{3,2},{4,5},{5,4},{6,7},{7,6},{8,16},{9,17},{10,... | collective-permute-start | bytes 983048 | tf_op jit(solution)/shard_map/ppermute | solution.py:436
  17.4 8.8 %collective-permute-start.5 = (f32[2,5,64,128]{3,2,1,0:T(8,128)S(1)}, f32[2,5,64,128]{3,2,1,0:T(8,128)S(1)}, u32[]{:S(2)}, u32[]{:S(2)}) collective-permute-start(f32[2,5,64,128]{3,2,1,0:T(8,128)S(1)} %get-tuple-element.26), channel_id=1, source_target_pairs={{0,8},{8,0},{16,24},{24,16},{32,40},{40,32},{48,56},{56,48},{64,72... | collective-permute-start | bytes 983048 | tf_op jit(solution)/shard_map/ppermute | solution.py:437
  17.4 8.8 %collective-permute-start.6 = (f32[2,5,64,128]{3,2,1,0:T(8,128)S(1)}, f32[2,5,64,128]{3,2,1,0:T(8,128)S(1)}, u32[]{:S(2)}, u32[]{:S(2)}) collective-permute-start(f32[2,5,64,128]{3,2,1,0:T(8,128)S(1)} %get-tuple-element.27), channel_id=1, source_target_pairs={{0,7},{1,2},{2,1},{3,4},{4,3},{5,6},{6,5},{7,0},{8,15},{9,10},{10,... | collective-permute-start | bytes 983048 | tf_op jit(solution)/shard_map/ppermute | solution.py:438
  19.7 6.4 %collective-permute-start.7 = (f32[2,5,64,128]{3,2,1,0:T(8,128)S(1)}, f32[2,5,64,128]{3,2,1,0:T(8,128)S(1)}, u32[]{:S(2)}, u32[]{:S(2)}) collective-permute-start(f32[2,5,64,128]{3,2,1,0:T(8,128)S(1)} %get-tuple-element.28), channel_id=1, source_target_pairs={{0,1},{1,0},{2,3},{3,2},{4,5},{5,4},{6,7},{7,6},{8,9},{9,8},{10,11... | collective-permute-start | bytes 983048 | tf_op jit(solution)/shard_map/ppermute | solution.py:439

commit v3 on v2

--- a/solution.py
+++ b/solution.py
@@ -101,23 +101,28 @@
             slots[1][t, f, rows(m), :] = two[f]
 
 
-def halo_pair(slots, sign, has, t, f, m, scale):
-    near = slots[0][t, f, rows(m), :]
-    far = jnp.where(has, slots[1][t, f, rows(m), :], 0.0)
-    return scale * (near + far), (scale * sign) * (near - far)
+def halo_sides(slots, has, t, f, masks, scale):
+    out = []
+    other = jnp.where(has, scale, 0.0)
+    for m in range(MODES):
+        near = (scale * masks[m]) * slots[0][t, f, rows(m), :]
+        far = (other * masks[m]) * slots[1][t, f, rows(m), :]
+        out.append([near + far, near - far])
+    return out
 
 
 def first_faces(*refs):
-    small, (modal, q0, coefs, x_even, x_odd, y_even, y_odd), (sums, sems, *held, small_sems) = refs[:5], refs[5:12], refs[12:]
+    small, (modal, q0, coefs, sums, x_even, x_odd, y_even, y_odd), (sems, *held, small_sems) = refs[:5], refs[5:13], refs[13:]
+    def copy(t, f):
+        return pltpu.make_async_copy(modal.at[f, :, :, pl.ds(t * LANES, LANES)], q0.at[t, f], sems.at[t, f])
+
+    for f in range(FIELDS):
+        copy(0, f).start()
     loads = [pltpu.make_async_copy(a, b, small_sems.at[i]) for i, (a, b) in enumerate(zip(small, held))]
     for load in loads:
         load.start()
-    def copy(t, f):
-        return pltpu.make_async_copy(modal.at[f, :, :, pl.ds(t * LANES, LANES)], q0.at[t, f], sems.at[t, f])
-
-    for t in range(TILES):
-        for f in range(FIELDS):
-            copy(t, f).start()
+    for f in range(FIELDS):
+        copy(1, f).start()
     (sign_x, _), (sign_y, _) = place()
     for load in loads:
         load.wait()
@@ -141,14 +146,14 @@
                         e1 = q if e1 is None else e1 + q
                     else:
                         o1 = q if o1 is None else o1 + q
-                sums[2, f, rows(a), :] = e1
-                sums[3, f, rows(a), :] = o1
+                sums[2, t, f, rows(a), :] = e1
+                sums[3, t, f, rows(a), :] = o1
             for b in range(MODES):
-                sums[0, f, rows(b), :] = e0[b]
-                sums[1, f, rows(b), :] = o0[b]
+                sums[0, t, f, rows(b), :] = e0[b]
+                sums[1, t, f, rows(b), :] = o0[b]
         coef = medium(coefs, t)
         for d, sign, slots in ((0, sign_x, (x_even, x_odd)), (1, sign_y, (y_even, y_odd))):
-            write_faces(d, sign, coef, sums, slots, t)
+            write_faces(d, sign, coef, sums.at[:, t], slots, t)
 
 
 def scaled(coef, d, s):
@@ -220,7 +225,7 @@
             sweep(2, loader(t), base_e, base_o, us, emit)
         return carry
 
-    lax.fori_loop(0, MODES, line, 0)
+    lax.fori_loop(0, MODES, line, 0, unroll=2)
 
 
 def second_direction(q, acc, coefs, metric, h):
@@ -242,7 +247,7 @@
             sweep(1, load, base_e, base_o, us, emit)
             return carry
 
-        lax.fori_loop(0, MODES, line, 0)
+        lax.fori_loop(0, MODES, line, 0, unroll=2)
 
 
 def first_direction(q, acc, coefs, metric, h, finish):
@@ -265,105 +270,93 @@
             sweep(0, load, base_e, base_o, us, emit)
             return carry
 
-        lax.fori_loop(0, MODES, line, 0)
-
-
-def local_rate(coefs, g0, g1, q0, r1, traces, acc):
+        lax.fori_loop(0, MODES, line, 0, unroll=2)
+
+
+def local_rate(coefs, g0, g1, sums, q0, r1, traces, acc):
     metric = g0[0], g1[0]
-    traces[pl.ds(2, 2)] = jnp.zeros((2,) + FACE, F32)
     third_direction(q0, acc, coefs, metric, TIME_STEP)
     second_direction(q0, acc, coefs, metric, TIME_STEP)
 
     def finish(t, b, a, totals, kept):
         level = coefs[t, LEVEL + jnp.maximum(a, b)]
-        slot = 2 + lax.rem(b, 2)
         for f in range(FIELDS):
             rate = level * totals[f]
             r1[t, f, a, rows(b), :] = rate
-            q = q0[t, f, a, rows(b), :] + SECTION_B1 * rate
-            kept[a % 2, f] = q if a < 2 else kept[a % 2, f] + q
-            traces[slot, t, f, rows(a), :] = traces[slot, t, f, rows(a), :] + q
+            kept[a % 2, f] = rate if a < 2 else kept[a % 2, f] + rate
         if a == MODES - 1:
             for (parity, f), total in kept.items():
-                traces[parity, t, f, rows(b), :] = total
+                traces[parity, t, f, rows(b), :] = sums[parity, t, f, rows(b), :] + SECTION_B1 * total
 
     first_direction(q0, acc, coefs, metric, TIME_STEP, finish)
+    for t in range(TILES):
+
+        def field(f, carry):
+            for a in range(MODES):
+                for parity in range(2):
+                    total = r1[t, f, a, rows(parity), :]
+                    for b in range(parity + 2, MODES, 2):
+                        total = total + r1[t, f, a, rows(b), :]
+                    traces[2 + parity, t, f, rows(a), :] = sums[2 + parity, t, f, rows(a), :] + SECTION_B1 * total
+            return carry
+
+        lax.fori_loop(0, FIELDS, field, 0)
 
 
 def second_faces(coefs, g0, g1, traces, xo, xe, yo, ye, x_even, x_odd, y_even, y_odd, sums):
+    (sign_x, has_x), (sign_y, has_y) = place()
+    s = SECTION_B1 * TIME_STEP
+    sides = (((xe, xo), has_x, s * g0[0]), ((ye, yo), has_y, s * g1[0]))
+    signs = (sign_x, sign_y)
+    for t in range(TILES):
+        mask = [coefs[t, LEVEL + k] for k in range(MODES)]
+        weights = [[coefs[t, WEIGHT], signs[d] * coefs[t, WEIGHT + 1]] for d in range(2)]
+        heavy = [[(m + 0.5) * mask[m] * (signs[1 - d] if m % 2 else 1.0) for m in range(MODES)] for d in range(2)]
+        for f in range(FIELDS):
+            pairs = [halo_sides(slots, has, t, f, mask, scale) for slots, has, scale in sides]
+            across = [
+                [
+                    [sum((pair[m][kind] for m in range(parity + 2, MODES, 2)), pair[parity][kind]) for parity in range(2)]
+                    for kind in range(2)
+                ]
+                for pair in pairs
+            ]
+            for d in range(2):
+                for m in range(MODES):
+                    for parity in range(2):
+                        sums[2 * d + parity, f, rows(m), :] = traces[2 * d + parity, t, f, rows(m), :] + (
+                            weights[d][parity] * pairs[d][m][parity] + heavy[d][m] * across[1 - d][m % 2][parity]
+                        )
+        coef = medium(coefs, t)
+        for d, slots in ((0, (x_even, x_odd)), (1, (y_even, y_odd))):
+            write_faces(d, signs[d], coef, sums, slots, t)
+
+
+def halo_terms(coefs, t, f, sides):
+    mask = [coefs[t, LEVEL + k] for k in range(MODES)]
+    plain = [(m + 0.5) * coefs[t, LIVE + m] for m in range(MODES)]
+    first, second = (halo_sides(slots, has, t, f, mask, scale) for slots, has, scale, _ in sides)
+    weights = [[(sides[d][3] if m % 2 else 1.0) * plain[m] for m in range(MODES)] for d in range(2)]
+    return lambda a, b: weights[0][a] * first[b][a % 2] + weights[1][b] * second[a][b % 2]
+
+
+def second_local(coefs, g0, g1, q0, r1, xo, xe, yo, ye, part, q1, acc):
     metric = g0[0], g1[0]
     (sign_x, has_x), (sign_y, has_y) = place()
-    sides = ((0, (xe, xo), sign_x, has_x), (1, (ye, yo), sign_y, has_y))
-
-    for t in range(TILES):
-        mask = [coefs[t, LEVEL + k] for k in range(MODES)]
-        weights = [coefs[t, WEIGHT + parity] for parity in range(2)]
-        scale = [SECTION_B1 * TIME_STEP * metric[d] for d in range(2)]
-
-        for f in range(FIELDS):
-            pairs = []
-            across = []
-            for d, slots, sign, has in sides:
-                pair = [
-                    [mask[m] * x for x in halo_pair(slots, sign, has, t, f, m, scale[d])] for m in range(MODES)
-                ]
-                pairs.append(pair)
-                across.append(
-                    [
-                        [sum(pair[m][kind] for m in range(parity + 2, MODES, 2)) + pair[parity][kind] for parity in range(2)]
-                        for kind in range(2)
-                    ]
-                )
-            for d in range(2):
-                for m in range(MODES):
-                    heavy = (m + 0.5) * mask[m]
-                    for parity in range(2):
-                        sums[2 * d + parity, f, rows(m), :] = traces[2 * d + parity, t, f, rows(m), :] + (
-                            weights[parity] * pairs[d][m][parity] + heavy * across[1 - d][m % 2][parity]
-                        )
-        coef = medium(coefs, t)
-        for d, sign, slots in ((0, sign_x, (x_even, x_odd)), (1, sign_y, (y_even, y_odd))):
-            write_faces(d, sign, coef, sums, slots, t)
-
-
-def store_halos(halo, xe, xo, ye, yo, metric, s):
-    (sign_x, has_x), (sign_y, has_y) = place()
-    for d, slots, sign, has in ((0, (xe, xo), sign_x, has_x), (1, (ye, yo), sign_y, has_y)):
-        for t in range(TILES):
-            scale = s * metric[d]
-
-            def one(f, carry):
-                for m in range(MODES):
-                    plus, minus = halo_pair(slots, sign, has, t, f, m, scale)
-                    halo[d, 0, t, f, rows(m), :] = plus
-                    halo[d, 1, t, f, rows(m), :] = minus
-                return carry
-
-            lax.fori_loop(0, FIELDS, one, 0)
-
-
-def halo_term(halo, t, f, a, b, weight, kind):
-    return (a + 0.5) * halo[0, a % 2, t, f, rows(b), :] + weight * halo[1, kind, t, f, rows(a), :]
-
-
-def second_local(coefs, g0, g1, q0, r1, xo, xe, yo, ye, part, q1, acc, halo):
-    metric = g0[0], g1[0]
-    store_halos(halo, xe, xo, ye, yo, metric, TIME_STEP)
-    for t in range(TILES):
-
-        def column(b, carry):
-            weight = b.astype(F32) + 0.5
-            kind = lax.rem(b, 2)
+    sides = (((xe, xo), has_x, TIME_STEP * metric[0], sign_x), ((ye, yo), has_y, TIME_STEP * metric[1], sign_y))
+    for t in range(TILES):
+
+        def field(f, carry):
+            term = halo_terms(coefs, t, f, sides)
             for a in range(MODES):
-                level = coefs[t, LEVEL + jnp.maximum(a, b)]
-                for f in range(FIELDS):
-                    rate = r1[t, f, a, rows(b), :] + level * halo_term(halo, t, f, a, b, weight, kind)
+                for b in range(MODES):
+                    rate = r1[t, f, a, rows(b), :] + term(a, b)
                     q = q0[t, f, a, rows(b), :] + SECTION_B1 * rate
                     q1[t, f, a, rows(b), :] = q
                     part[t, f, a, rows(b), :] = q + (SECTION_B2 * SECTION_A2) * rate
             return carry
 
-        lax.fori_loop(0, MODES, column, 0)
+        lax.fori_loop(0, FIELDS, field, 0)
     third_direction(q1, acc, coefs, metric, SECTION_B2 * TIME_STEP)
     second_direction(q1, acc, coefs, metric, SECTION_B2 * TIME_STEP)
 
@@ -376,30 +369,20 @@
 
 
 def last_add(coefs, g0, g1, part, xo, xe, yo, ye, out, done, sems):
-    metric = g0[0], g1[0]
     (sign_x, has_x), (sign_y, has_y) = place()
-    sides = ((0, (xe, xo), sign_x, has_x), (1, (ye, yo), sign_y, has_y))
+    s = SECTION_B2 * TIME_STEP
+    sides = (((xe, xo), has_x, s * g0[0], sign_x), ((ye, yo), has_y, s * g1[0], sign_y))
 
     def copy(t, f):
         lanes = pl.ds(pl.multiple_of(t * LANES, LANES), LANES)
         return pltpu.make_async_copy(done.at[t, f], out.at[f, :, :, lanes], sems.at[t, f])
 
     def tile(t, carry):
-        mask = [coefs[t, LEVEL + k] for k in range(MODES)]
-        weight = [(m + 0.5) * coefs[t, LIVE + m] for m in range(MODES)]
-
         def field(f, carry):
-            first, second = (
-                [
-                    [mask[m] * x for x in halo_pair(slots, sign, has, t, f, m, SECTION_B2 * TIME_STEP * metric[d])]
-                    for m in range(MODES)
-                ]
-                for d, slots, sign, has in sides
-            )
+            term = halo_terms(coefs, t, f, sides)
             for a in range(MODES):
                 for b in range(MODES):
-                    term = weight[a] * first[b][a % 2] + weight[b] * second[a][b % 2]
-                    done[t, f, a, rows(b), :] = part[t, f, a, rows(b), :] + term
+                    done[t, f, a, rows(b), :] = part[t, f, a, rows(b), :] + term(a, b)
             copy(t, f).start()
             return carry
 
@@ -465,13 +448,13 @@
     bulk = jax.ShapeDtypeStruct(BULK, F32)
     sems = pltpu.SemaphoreType.DMA((TILES, FIELDS))
     plane = (FIELDS, MODES * MODES, LANES)
-    q0, coefs, *faces = call(
+    q0, coefs, sums, *faces = call(
         first_faces,
         tuple(pltpu.with_memory_space_constraint(x, pltpu.HBM) for x in (*small, modal)),
         [FAR] * 6,
-        (bulk, jax.ShapeDtypeStruct(COEFS, F32)) + (face,) * 4,
-        (LOCAL,) * 6,
-        [pltpu.VMEM((4,) + plane, F32), sems]
+        (bulk, jax.ShapeDtypeStruct(COEFS, F32), jax.ShapeDtypeStruct((4,) + FACE, F32)) + (face,) * 4,
+        (LOCAL,) * 7,
+        [sems]
         + [pltpu.VMEM(x.shape, x.dtype) for x in small]
         + [pltpu.SemaphoreType.DMA((len(small),))],
         2_000_000,
@@ -479,8 +462,8 @@
     halos = swap(faces)
     r1, traces = call(
         local_rate,
-        (coefs, g0, g1, q0),
-        [LOCAL, SCALAR, SCALAR, LOCAL],
+        (coefs, g0, g1, sums, q0),
+        [LOCAL, SCALAR, SCALAR, LOCAL, LOCAL],
         (bulk, jax.ShapeDtypeStruct((4,) + FACE, F32)),
         (LOCAL,) * 2,
         [pltpu.VMEM(BULK, F32)],
@@ -496,14 +479,13 @@
         2_000_000,
     )
     last = swap(faces)
-    halo = pltpu.VMEM((2, 2) + FACE, F32)
     part = call(
         second_local,
         (coefs, g0, g1, q0, r1, *halos),
         [LOCAL, SCALAR, SCALAR] + [LOCAL] * 6,
         bulk,
         LOCAL,
-        [pltpu.VMEM(BULK, F32), pltpu.VMEM(BULK, F32), halo],
+        [pltpu.VMEM(BULK, F32), pltpu.VMEM(BULK, F32)],
         20_000_000,
     )
     out = call(

time: 28 us -> 27.6 us (0.986)
  Pallas kernels: 12.4 us -> 11.4 us
  waiting for transfers between devices: 3.06 us -> 3.61 us
    pallas_call x5, Pallas kernels: 12.4 us -> 11.4 us  [call(): pl.pallas_call(body, out_shape=outs, in_specs=specs, out_specs=out_specs,...]
    ppermute x2, waiting for transfers between devices: 2.5 us -> 3.05 us  [exchange(): lax.ppermute(x_odd, both, dom_perms[1])]
  transfers between devices with their start and end apart: 8 -> 8, of which waited for: 3 -> 3; matrix products, arithmetic and copies ran while one was open for 0% -> 0% of each run, Pallas kernels for 29% -> 26%
where the time goes in v3:
time: 27.6 us; the launch traced here: 27.4 us
  Pallas kernels  11.4 us (41%)
  starting transfers between devices  11 us (40%)
  waiting for transfers between devices  3.61 us (13%)
  between operations  1.34 us (5%)
    pallas_call x5, Pallas kernels, call(): pl.pallas_call(body, out_shape=outs, in_specs=specs, out_specs=out_specs,...  11.4 us
    ppermute x2, starting transfers between devices, exchange(): lax.ppermute(x_odd, both, dom_perms[1])  5.5 us
    ppermute x2, starting transfers between devices, exchange(): lax.ppermute(y_odd, 'grp', grp_perms[1])  5.48 us
    ppermute x2, waiting for transfers between devices, exchange(): lax.ppermute(x_odd, both, dom_perms[1])  3.05 us
  transfers between devices with their start and end apart: 8, of which 3 were waited for; matrix products, arithmetic and copies ran while one was open for 0% of the time, Pallas kernels for 26%

profile of v3, /device:TPU:24, one launch (start us, length us, event | category | flops | bytes accessed | tf_op | source)
XLA Modules:
  0.0 27.4 jit_solution(10939430417067825829)
XLA Ops:
  0.0 2.1 %first_faces.1 = (f32[2,5,8,64,128]{4,3,2,1,0:T(8,128)S(1)}, f32[2,25,8,128]{3,2,1,0:T(8,128)S(1)}, f32[4,2,5,64,128]{4,3,2,1,0:T(8,128)S(1)}, f32[2,5,64,128]{3...) custom-call(f32[3,256]{1,0:T(4,128)} %refs_0_.1, ...), custom_call_target="tpu_custom_call" | custom-call | flops 2000000 | bytes 2600000 | tf_op jit(solution)/shard_map/first_faces/pallas_call | solution.py:403
  2.1 3.0 %collective-permute-start = (f32[2,5,64,128]{3,2,1,0:T(8,128)S(1)}, f32[2,5,64,128]{3,2,1,0:T(8,128)S(1)}, u32[]{:S(2)}, u32[]{:S(2)}) collective-permute-start(f32[2,5,64,128]{3,2,1,0:T(8,128)S(1)} %get-tuple-element.22), channel_id=1, source_target_pairs={{0,1},{1,0},{2,3},{3,2},{4,5},{5,4},{6,7},{7,6},{8,16},{9,17},{10,... | collective-permute-start | bytes 983048 | tf_op jit(solution)/shard_map/ppermute | solution.py:419
  5.2 0.0 collective-permute-start.1
  5.2 3.2 %collective-permute-start.2 = (f32[2,5,64,128]{3,2,1,0:T(8,128)S(1)}, f32[2,5,64,128]{3,2,1,0:T(8,128)S(1)}, u32[]{:S(2)}, u32[]{:S(2)}) collective-permute-start(f32[2,5,64,128]{3,2,1,0:T(8,128)S(1)} %get-tuple-element.24), channel_id=1, source_target_pairs={{0,7},{1,2},{2,1},{3,4},{4,3},{5,6},{6,5},{7,0},{8,15},{9,10},{10,... | collective-permute-start | bytes 983048 | tf_op jit(solution)/shard_map/ppermute | solution.py:421
  8.4 0.0 collective-permute-start.3
  9.7 3.2 %local_rate.1 = (f32[2,5,8,64,128]{4,3,2,1,0:T(8,128)S(1)}, f32[4,2,5,64,128]{4,3,2,1,0:T(8,128)S(1)}) custom-call(f32[2,25,8,128]{3,2,1,0:T(8,128)S(1)} %get-tuple-element.18.coefs, f32[1]{0:T(128)S(6)} %copy.9.g0, f32[1]{0:T(128)S(6)} %copy.10.g1, f32[4,2,5,64,128]{4,3,2,1,0:T(8,128)S(1)} %get-tuple-element.20.sums, ...), custom_call_target="tpu_custom_call" | custom-call | flops 16000000 | bytes 2600000 | tf_op jit(solution)/shard_map/local_rate/pallas_call | solution.py:403
  12.8 0.9 %collective-permute-done.xo = f32[2,5,64,128]{3,2,1,0:T(8,128)S(1)} collective-permute-done((f32[2,5,64,128]{3,2,1,0:T(8,128)S(1)}, f32[2,5,64,128]{3,2,1,0:T(8,128)S(1)}, u32[]{:S(2)}, u32[]{:S(2)}) %collective-permute-start) | collective-permute-done | bytes 327712 | tf_op jit(solution)/shard_map/ppermute | solution.py:419
  13.8 0.5 %collective-permute-done.1.xe = f32[2,5,64,128]{3,2,1,0:T(8,128)S(1)} collective-permute-done((f32[2,5,64,128]{3,2,1,0:T(8,128)S(1)}, f32[2,5,64,128]{3,2,1,0:T(8,128)S(1)}, u32[]{:S(2)}, u32[]{:S(2)}) %collective-permute-start.1) | collective-permute-done | bytes 327712 | tf_op jit(solution)/shard_map/ppermute | solution.py:420
  14.3 0.0 collective-permute-done.2.yo
  14.3 0.0 collective-permute-done.3.ye
  14.3 0.5 %second_faces.1 = (f32[2,5,64,128]{3,2,1,0:T(8,128)S(1)}, f32[2,5,64,128]{3,2,1,0:T(8,128)S(1)}, f32[2,5,64,128]{3,2,1,0:T(8,128)S(1)}, f32[2,5,64,128]{3,2,1,0:T(8,128)S(1)}) custom-call(f32[2,25,8,128]{3,2,1,0:T(8,128)S(1)} %get-tuple-element.18.coefs, f32[1]{0:T(128)S(6)} %copy.9.g0, f32[1]{0:T(128)S(6)} %copy.10.g1, ...), custom_call_target="tpu_custom_call" | custom-call | flops 2000000 | bytes 2600000 | tf_op jit(solution)/shard_map/second_faces/pallas_call | solution.py:403
  14.9 2.5 %collective-permute-start.4 = (f32[2,5,64,128]{3,2,1,0:T(8,128)S(1)}, f32[2,5,64,128]{3,2,1,0:T(8,128)S(1)}, u32[]{:S(2)}, u32[]{:S(2)}) collective-permute-start(f32[2,5,64,128]{3,2,1,0:T(8,128)S(1)} %get-tuple-element.27), channel_id=1, source_target_pairs={{0,1},{1,0},{2,3},{3,2},{4,5},{5,4},{6,7},{7,6},{8,16},{9,17},{10,... | collective-permute-start | bytes 983048 | tf_op jit(solution)/shard_map/ppermute | solution.py:419
  17.4 0.0 collective-permute-start.5
  17.4 2.3 %collective-permute-start.6 = (f32[2,5,64,128]{3,2,1,0:T(8,128)S(1)}, f32[2,5,64,128]{3,2,1,0:T(8,128)S(1)}, u32[]{:S(2)}, u32[]{:S(2)}) collective-permute-start(f32[2,5,64,128]{3,2,1,0:T(8,128)S(1)} %get-tuple-element.29), channel_id=1, source_target_pairs={{0,7},{1,2},{2,1},{3,4},{4,3},{5,6},{6,5},{7,0},{8,15},{9,10},{10,... | collective-permute-start | bytes 983048 | tf_op jit(solution)/shard_map/ppermute | solution.py:421
  19.7 0.0 collective-permute-start.7
  19.7 3.9 %second_local.1.part = f32[2,5,8,64,128]{4,3,2,1,0:T(8,128)S(1)} custom-call(f32[2,25,8,128]{3,2,1,0:T(8,128)S(1)} %get-tuple-element.18.coefs, f32[1]{0:T(128)S(6)} %copy.9.g0, f32[1]{0:T(128)S(6)} %copy.10.g1, f32[2,5,8,64,128]{4,3,2,1,0:T(8,128)S(1)} %get-tuple-element.19.q0, f32[2,5,8,64,128]{4,3,2,1,0:T(8,128)S(1)} %get-tuple-element.21.r1, ...), custom_call_target="tpu_custom_call" | custom-call | flops 20000000 | bytes 2600000 | tf_op jit(solution)/shard_map/second_local/pallas_call | solution.py:403
  23.7 2.1 %collective-permute-done.4.xo = f32[2,5,64,128]{3,2,1,0:T(8,128)S(1)} collective-permute-done((f32[2,5,64,128]{3,2,1,0:T(8,128)S(1)}, f32[2,5,64,128]{3,2,1,0:T(8,128)S(1)}, u32[]{:S(2)}, u32[]{:S(2)}) %collective-permute-start.4) | collective-permute-done | bytes 327712 | tf_op jit(solution)/shard_map/ppermute | solution.py:419
  25.8 0.0 collective-permute-done.5.xe
  25.8 0.0 collective-permute-done.6.yo
  25.8 0.0 collective-permute-done.7.ye
  25.8 1.6 %last_add.1 = f32[5,8,64,256]{3,2,1,0:T(8,128)} custom-call(f32[2,25,8,128]{3,2,1,0:T(8,128)S(1)} %get-tuple-element.18.coefs, f32[1]{0:T(128)S(6)} %copy.9.g0, f32[1]{0:T(128)S(6)} %copy.10.g1, f32[2,5,8,64,128]{4,3,2,1,0:T(8,128)S(1)} %second_local.1.part, f32[2,5,64,128]{3,2,1,0:T(8,128)S(1)} %collective-permute-done.4.xo, ...), custom_call_target="tpu_custom_call" | custom-call | flops 4000000 | bytes 2600000 | tf_op jit(solution)/shard_map/last_add/pallas_call | solution.py:403
Async XLA Ops:
  2.1 11.6 %collective-permute-start = (f32[2,5,64,128]{3,2,1,0:T(8,128)S(1)}, f32[2,5,64,128]{3,2,1,0:T(8,128)S(1)}, u32[]{:S(2)}, u32[]{:S(2)}) collective-permute-start(f32[2,5,64,128]{3,2,1,0:T(8,128)S(1)} %get-tuple-element.22), channel_id=1, source_target_pairs={{0,1},{1,0},{2,3},{3,2},{4,5},{5,4},{6,7},{7,6},{8,16},{9,17},{10,... | collective-permute-start | bytes 983048 | tf_op jit(solution)/shard_map/ppermute | solution.py:419
  5.2 9.2 %collective-permute-start.1 = (f32[2,5,64,128]{3,2,1,0:T(8,128)S(1)}, f32[2,5,64,128]{3,2,1,0:T(8,128)S(1)}, u32[]{:S(2)}, u32[]{:S(2)}) collective-permute-start(f32[2,5,64,128]{3,2,1,0:T(8,128)S(1)} %get-tuple-element.23), channel_id=1, source_target_pairs={{0,8},{8,0},{16,24},{24,16},{32,40},{40,32},{48,56},{56,48},{64,72... | collective-permute-start | bytes 983048 | tf_op jit(solution)/shard_map/ppermute | solution.py:420
  5.2 9.1 %collective-permute-start.2 = (f32[2,5,64,128]{3,2,1,0:T(8,128)S(1)}, f32[2,5,64,128]{3,2,1,0:T(8,128)S(1)}, u32[]{:S(2)}, u32[]{:S(2)}) collective-permute-start(f32[2,5,64,128]{3,2,1,0:T(8,128)S(1)} %get-tuple-element.24), channel_id=1, source_target_pairs={{0,7},{1,2},{2,1},{3,4},{4,3},{5,6},{6,5},{7,0},{8,15},{9,10},{10,... | collective-permute-start | bytes 983048 | tf_op jit(solution)/shard_map/ppermute | solution.py:421
  8.4 6.0 %collective-permute-start.3 = (f32[2,5,64,128]{3,2,1,0:T(8,128)S(1)}, f32[2,5,64,128]{3,2,1,0:T(8,128)S(1)}, u32[]{:S(2)}, u32[]{:S(2)}) collective-permute-start(f32[2,5,64,128]{3,2,1,0:T(8,128)S(1)} %get-tuple-element.25), channel_id=1, source_target_pairs={{0,1},{1,0},{2,3},{3,2},{4,5},{5,4},{6,7},{7,6},{8,9},{9,8},{10,11... | collective-permute-start | bytes 983048 | tf_op jit(solution)/shard_map/ppermute | solution.py:422
  14.9 10.9 %collective-permute-start.4 = (f32[2,5,64,128]{3,2,1,0:T(8,128)S(1)}, f32[2,5,64,128]{3,2,1,0:T(8,128)S(1)}, u32[]{:S(2)}, u32[]{:S(2)}) collective-permute-start(f32[2,5,64,128]{3,2,1,0:T(8,128)S(1)} %get-tuple-element.27), channel_id=1, source_target_pairs={{0,1},{1,0},{2,3},{3,2},{4,5},{5,4},{6,7},{7,6},{8,16},{9,17},{10,... | collective-permute-start | bytes 983048 | tf_op jit(solution)/shard_map/ppermute | solution.py:419
  17.4 8.4 %collective-permute-start.5 = (f32[2,5,64,128]{3,2,1,0:T(8,128)S(1)}, f32[2,5,64,128]{3,2,1,0:T(8,128)S(1)}, u32[]{:S(2)}, u32[]{:S(2)}) collective-permute-start(f32[2,5,64,128]{3,2,1,0:T(8,128)S(1)} %get-tuple-element.28), channel_id=1, source_target_pairs={{0,8},{8,0},{16,24},{24,16},{32,40},{40,32},{48,56},{56,48},{64,72... | collective-permute-start | bytes 983048 | tf_op jit(solution)/shard_map/ppermute | solution.py:420
  17.4 8.4 %collective-permute-start.6 = (f32[2,5,64,128]{3,2,1,0:T(8,128)S(1)}, f32[2,5,64,128]{3,2,1,0:T(8,128)S(1)}, u32[]{:S(2)}, u32[]{:S(2)}) collective-permute-start(f32[2,5,64,128]{3,2,1,0:T(8,128)S(1)} %get-tuple-element.29), channel_id=1, source_target_pairs={{0,7},{1,2},{2,1},{3,4},{4,3},{5,6},{6,5},{7,0},{8,15},{9,10},{10,... | collective-permute-start | bytes 983048 | tf_op jit(solution)/shard_map/ppermute | solution.py:421
  19.7 6.1 %collective-permute-start.7 = (f32[2,5,64,128]{3,2,1,0:T(8,128)S(1)}, f32[2,5,64,128]{3,2,1,0:T(8,128)S(1)}, u32[]{:S(2)}, u32[]{:S(2)}) collective-permute-start(f32[2,5,64,128]{3,2,1,0:T(8,128)S(1)} %get-tuple-element.30), channel_id=1, source_target_pairs={{0,1},{1,0},{2,3},{3,2},{4,5},{5,4},{6,7},{7,6},{8,9},{9,8},{10,11... | collective-permute-start | bytes 983048 | tf_op jit(solution)/shard_map/ppermute | solution.py:422

commit v4 on v3

--- a/solution.py
+++ b/solution.py
@@ -112,7 +112,8 @@
 
 
 def first_faces(*refs):
-    small, (modal, q0, coefs, sums, x_even, x_odd, y_even, y_odd), (sems, *held, small_sems) = refs[:5], refs[5:13], refs[13:]
+    small, (modal, q0, coefs, sums, x_even, x_odd), (sems, *held, small_sems) = refs[:5], refs[5:11], refs[11:]
+
     def copy(t, f):
         return pltpu.make_async_copy(modal.at[f, :, :, pl.ds(t * LANES, LANES)], q0.at[t, f], sems.at[t, f])
 
@@ -123,7 +124,7 @@
         load.start()
     for f in range(FIELDS):
         copy(1, f).start()
-    (sign_x, _), (sign_y, _) = place()
+    (sign_x, _), _ = place()
     for load in loads:
         load.wait()
     store_coefs(coefs, *held)
@@ -151,9 +152,13 @@
             for b in range(MODES):
                 sums[0, t, f, rows(b), :] = e0[b]
                 sums[1, t, f, rows(b), :] = o0[b]
-        coef = medium(coefs, t)
-        for d, sign, slots in ((0, sign_x, (x_even, x_odd)), (1, sign_y, (y_even, y_odd))):
-            write_faces(d, sign, coef, sums.at[:, t], slots, t)
+        write_faces(0, sign_x, medium(coefs, t), sums.at[:, t], (x_even, x_odd), t)
+
+
+def first_grp_faces(coefs, sums, y_even, y_odd):
+    _, (sign_y, _) = place()
+    for t in range(TILES):
+        write_faces(1, sign_y, medium(coefs, t), sums.at[:, t], (y_even, y_odd), t)
 
 
 def scaled(coef, d, s):
@@ -303,33 +308,41 @@
         lax.fori_loop(0, FIELDS, field, 0)
 
 
-def second_faces(coefs, g0, g1, traces, xo, xe, yo, ye, x_even, x_odd, y_even, y_odd, sums):
+def second_faces(d, coefs, g0, g1, traces, xo, xe, yo, ye, even, odd, sums, table=None):
     (sign_x, has_x), (sign_y, has_y) = place()
     s = SECTION_B1 * TIME_STEP
     sides = (((xe, xo), has_x, s * g0[0]), ((ye, yo), has_y, s * g1[0]))
     signs = (sign_x, sign_y)
     for t in range(TILES):
         mask = [coefs[t, LEVEL + k] for k in range(MODES)]
-        weights = [[coefs[t, WEIGHT], signs[d] * coefs[t, WEIGHT + 1]] for d in range(2)]
-        heavy = [[(m + 0.5) * mask[m] * (signs[1 - d] if m % 2 else 1.0) for m in range(MODES)] for d in range(2)]
+        live = coefs.at[t, pl.ds(WEIGHT, 2)] if table is None else table.at[t]
+        weights = live[0], signs[d] * live[1]
+        heavy = [(m + 0.5) * mask[m] * (signs[1 - d] if m % 2 else 1.0) for m in range(MODES)]
         for f in range(FIELDS):
-            pairs = [halo_sides(slots, has, t, f, mask, scale) for slots, has, scale in sides]
+            along, other = (
+                halo_sides(slots, has, t, f, mask, scale) for slots, has, scale in (sides[d], sides[1 - d])
+            )
             across = [
-                [
-                    [sum((pair[m][kind] for m in range(parity + 2, MODES, 2)), pair[parity][kind]) for parity in range(2)]
-                    for kind in range(2)
-                ]
-                for pair in pairs
+                [sum((other[m][kind] for m in range(parity + 2, MODES, 2)), other[parity][kind]) for parity in range(2)]
+                for kind in range(2)
             ]
-            for d in range(2):
-                for m in range(MODES):
-                    for parity in range(2):
-                        sums[2 * d + parity, f, rows(m), :] = traces[2 * d + parity, t, f, rows(m), :] + (
-                            weights[d][parity] * pairs[d][m][parity] + heavy[d][m] * across[1 - d][m % 2][parity]
-                        )
-        coef = medium(coefs, t)
-        for d, slots in ((0, (x_even, x_odd)), (1, (y_even, y_odd))):
-            write_faces(d, signs[d], coef, sums, slots, t)
+            for m in range(MODES):
+                for parity in range(2):
+                    sums[2 * d + parity, f, rows(m), :] = traces[2 * d + parity, t, f, rows(m), :] + (
+                        weights[parity] * along[m][parity] + heavy[m] * across[m % 2][parity]
+                    )
+        write_faces(d, signs[d], medium(coefs, t), sums, (even, odd), t)
+
+
+def second_dom_faces(*refs):
+    *refs, weights, sums = refs
+    for t in range(TILES):
+        weights[t] = refs[0][t, pl.ds(WEIGHT, 2)]
+    second_faces(0, *refs, sums)
+
+
+def second_grp_faces(weights, *refs):
+    second_faces(1, *refs, weights)
 
 
 def halo_terms(coefs, t, f, sides):
@@ -448,18 +461,19 @@
     bulk = jax.ShapeDtypeStruct(BULK, F32)
     sems = pltpu.SemaphoreType.DMA((TILES, FIELDS))
     plane = (FIELDS, MODES * MODES, LANES)
-    q0, coefs, sums, *faces = call(
+    q0, coefs, sums, *x_faces = call(
         first_faces,
         tuple(pltpu.with_memory_space_constraint(x, pltpu.HBM) for x in (*small, modal)),
         [FAR] * 6,
-        (bulk, jax.ShapeDtypeStruct(COEFS, F32), jax.ShapeDtypeStruct((4,) + FACE, F32)) + (face,) * 4,
-        (LOCAL,) * 7,
+        (bulk, jax.ShapeDtypeStruct(COEFS, F32), jax.ShapeDtypeStruct((4,) + FACE, F32)) + (face,) * 2,
+        (LOCAL,) * 5,
         [sems]
         + [pltpu.VMEM(x.shape, x.dtype) for x in small]
         + [pltpu.SemaphoreType.DMA((len(small),))],
         2_000_000,
     )
-    halos = swap(faces)
+    y_faces = call(first_grp_faces, (coefs, sums), [LOCAL] * 2, (face,) * 2, (LOCAL,) * 2, [], 200_000)
+    halos = swap((*x_faces, *y_faces))
     r1, traces = call(
         local_rate,
         (coefs, g0, g1, sums, q0),
@@ -469,16 +483,22 @@
         [pltpu.VMEM(BULK, F32)],
         16_000_000,
     )
-    faces = call(
-        second_faces,
-        (coefs, g0, g1, traces, *halos),
-        [LOCAL, SCALAR, SCALAR] + [LOCAL] * 5,
-        (face,) * 4,
-        (LOCAL,) * 4,
-        [pltpu.VMEM((4,) + plane, F32)],
-        2_000_000,
-    )
-    last = swap(faces)
+    made = (coefs, g0, g1, traces, *halos)
+    specs = [LOCAL, SCALAR, SCALAR] + [LOCAL] * 5
+    work = [pltpu.VMEM((4,) + plane, F32)]
+    *x_faces, weights = call(
+        second_dom_faces,
+        made,
+        specs,
+        (face, face, jax.ShapeDtypeStruct((TILES, 2, MODES, LANES), F32)),
+        (LOCAL,) * 3,
+        work,
+        1_000_000,
+    )
+    y_faces = call(
+        second_grp_faces, (weights, *made), [LOCAL] + specs, (face,) * 2, (LOCAL,) * 2, work, 1_000_000
+    )
+    last = swap((*x_faces, *y_faces))
     part = call(
         second_local,
         (coefs, g0, g1, q0, r1, *halos),

time: 27.6 us -> 27.5 us (level)
  waiting for transfers between devices: 3.61 us -> 3.22 us
    ppermute x2, waiting for transfers between devices: 3.05 us -> 2.66 us  [exchange(): lax.ppermute(x_odd, both, dom_perms[1])]
    pallas_call x5 -> x7, Pallas kernels: 11.4 us -> 11.5 us  [call(): pl.pallas_call(body, out_shape=outs, in_specs=specs, out_specs=out_specs,...]
  transfers between devices with their start and end apart: 8 -> 8, of which waited for: 3 -> 3; matrix products, arithmetic and copies ran while one was open for 0% -> 0% of each run, Pallas kernels for 26% -> 27%
where the time goes in v4:
time: 27.5 us; the launch traced here: 27.3 us
  Pallas kernels  11.5 us (42%)
  starting transfers between devices  11.2 us (41%)
  waiting for transfers between devices  3.22 us (12%)
  between operations  1.35 us (5%)
    pallas_call x7, Pallas kernels, call(): pl.pallas_call(body, out_shape=outs, in_specs=specs, out_specs=out_specs,...  11.5 us
    ppermute x2, starting transfers between devices, exchange(): lax.ppermute(y_odd, 'grp', grp_perms[1])  5.64 us
    ppermute x2, starting transfers between devices, exchange(): lax.ppermute(x_odd, both, dom_perms[1])  5.5 us
    ppermute x2, waiting for transfers between devices, exchange(): lax.ppermute(x_odd, both, dom_perms[1])  2.66 us
    ppermute x2, waiting for transfers between devices, exchange(): lax.ppermute(x_even, 'dom', dom_perms[0])  0.55 us
  transfers between devices with their start and end apart: 8, of which 3 were waited for; matrix products, arithmetic and copies ran while one was open for 0% of the time, Pallas kernels for 27%

profile of v4, /device:TPU:24, one launch (start us, length us, event | category | flops | bytes accessed | tf_op | source)
XLA Modules:
  0.0 27.3 jit_solution(6615031670821517493)
XLA Ops:
  0.0 2.0 %first_faces.1 = (f32[2,5,8,64,128]{4,3,2,1,0:T(8,128)S(1)}, f32[2,25,8,128]{3,2,1,0:T(8,128)S(1)}, f32[4,2,5,64,128]{4,3,2,1,0:T(8,128)S(1)}, f32[2,5,64,128]{3,2,1,0:T(8,128)S(1)}, f32[2,5,64,128]{3,2,1,0:T(8,128)S(1)}) custom-call(f32[3,256]{1,0:T(4,128)} %refs_0_.1, f32[256]{0:T(256)} %refs_1_.3, f32[256]{0:T(256)} %refs_2_.3, f32[256]{0:T(256)} %refs_3_.1, ...), custom_call_target="tpu_custom_call" | custom-call | flops 2000000 | bytes 2600000 | tf_op jit(solution)/shard_map/first_faces/pallas_call | solution.py:416
  2.1 3.0 %collective-permute-start = (f32[2,5,64,128]{3,2,1,0:T(8,128)S(1)}, f32[2,5,64,128]{3,2,1,0:T(8,128)S(1)}, u32[]{:S(2)}, u32[]{:S(2)}) collective-permute-start(f32[2,5,64,128]{3,2,1,0:T(8,128)S(1)} %get-tuple-element.23), channel_id=1, source_target_pairs={{0,1},{1,0},{2,3},{3,2},{4,5},{5,4},{6,7},{7,6},{8,16},{9,17},{10,... | collective-permute-start | bytes 983048 | tf_op jit(solution)/shard_map/ppermute | solution.py:432
  5.1 0.0 collective-permute-start.1
  5.1 0.1 first_grp_faces.1
  5.2 3.2 %collective-permute-start.2 = (f32[2,5,64,128]{3,2,1,0:T(8,128)S(1)}, f32[2,5,64,128]{3,2,1,0:T(8,128)S(1)}, u32[]{:S(2)}, u32[]{:S(2)}) collective-permute-start(f32[2,5,64,128]{3,2,1,0:T(8,128)S(1)} %get-tuple-element.25), channel_id=1, source_target_pairs={{0,7},{1,2},{2,1},{3,4},{4,3},{5,6},{6,5},{7,0},{8,15},{9,10},{10,... | collective-permute-start | bytes 983048 | tf_op jit(solution)/shard_map/ppermute | solution.py:434
  8.5 0.0 collective-permute-start.3
  9.8 3.1 %local_rate.1 = (f32[2,5,8,64,128]{4,3,2,1,0:T(8,128)S(1)}, f32[4,2,5,64,128]{4,3,2,1,0:T(8,128)S(1)}) custom-call(f32[2,25,8,128]{3,2,1,0:T(8,128)S(1)} %get-tuple-element.19.coefs.refs_0_, f32[1]{0:T(128)S(6)} %copy.9.g0.refs_1_, f32[1]{0:T(128)S(6)} %copy.10.g1.refs_2_, f32[4,2,5,64,128]{4,3,2,1,0:T(8,128)S(1)} %get-tuple-element.21.sums, ...), custom_call_target="tpu_custom_call" | custom-call | flops 16000000 | bytes 2600000 | tf_op jit(solution)/shard_map/local_rate/pallas_call | solution.py:416
  12.9 0.8 %collective-permute-done.xo.refs_4_ = f32[2,5,64,128]{3,2,1,0:T(8,128)S(1)} collective-permute-done((f32[2,5,64,128]{3,2,1,0:T(8,128)S(1)}, f32[2,5,64,128]{3,2,1,0:T(8,128)S(1)}, u32[]{:S(2)}, u32[]{:S(2)}) %collective-permute-start) | collective-permute-done | bytes 327712 | tf_op jit(solution)/shard_map/ppermute | solution.py:432
  13.7 0.5 %collective-permute-done.1.xe.refs_5_ = f32[2,5,64,128]{3,2,1,0:T(8,128)S(1)} collective-permute-done((f32[2,5,64,128]{3,2,1,0:T(8,128)S(1)}, f32[2,5,64,128]{3,2,1,0:T(8,128)S(1)}, u32[]{:S(2)}, u32[]{:S(2)}) %collective-permute-start.1) | collective-permute-done | bytes 327712 | tf_op jit(solution)/shard_map/ppermute | solution.py:433
  14.2 0.0 collective-permute-done.2.yo.refs_6_
  14.2 0.0 collective-permute-done.3.ye.refs_7_
  14.3 0.3 %second_dom_faces.1 = (f32[2,5,64,128]{3,2,1,0:T(8,128)S(1)}, f32[2,5,64,128]{3,2,1,0:T(8,128)S(1)}, f32[2,2,8,128]{3,2,1,0:T(8,128)S(1)}) custom-call(f32[2,25,8,128]{3,2,1,0:T(8,128)S(1)} %get-tuple-element.19.coefs.refs_0_, f32[1]{0:T(128)S(6)} %copy.9.g0.refs_1_, f32[1]{0:T(128)S(6)} %copy.10.g1.refs_2_, ...), custom_call_target="tpu_custom_call" | custom-call | flops 1000000 | bytes 2600000 | tf_op jit(solution)/shard_map/second_dom_faces/pallas_call | solution.py:416
  14.6 2.5 %collective-permute-start.4 = (f32[2,5,64,128]{3,2,1,0:T(8,128)S(1)}, f32[2,5,64,128]{3,2,1,0:T(8,128)S(1)}, u32[]{:S(2)}, u32[]{:S(2)}) collective-permute-start(f32[2,5,64,128]{3,2,1,0:T(8,128)S(1)} %get-tuple-element.28), channel_id=1, source_target_pairs={{0,1},{1,0},{2,3},{3,2},{4,5},{5,4},{6,7},{7,6},{8,16},{9,17},{10,... | collective-permute-start | bytes 983048 | tf_op jit(solution)/shard_map/ppermute | solution.py:432
  17.1 0.0 collective-permute-start.5
  17.1 0.3 %second_grp_faces.1 = (f32[2,5,64,128]{3,2,1,0:T(8,128)S(1)}, f32[2,5,64,128]{3,2,1,0:T(8,128)S(1)}) custom-call(f32[2,2,8,128]{3,2,1,0:T(8,128)S(1)} %get-tuple-element.30.weights, f32[2,25,8,128]{3,2,1,0:T(8,128)S(1)} %get-tuple-element.19.coefs.refs_0_, f32[1]{0:T(128)S(6)} %copy.9.g0.refs_1_, f32[1]{0:T(128)S(6)} %copy.10.g1.refs_2_, ...), custom_call_target="tpu_custom_call" | custom-call | flops 1000000 | bytes 2600000 | tf_op jit(solution)/shard_map/second_grp_faces/pallas_call | solution.py:416
  17.4 2.4 %collective-permute-start.6 = (f32[2,5,64,128]{3,2,1,0:T(8,128)S(1)}, f32[2,5,64,128]{3,2,1,0:T(8,128)S(1)}, u32[]{:S(2)}, u32[]{:S(2)}) collective-permute-start(f32[2,5,64,128]{3,2,1,0:T(8,128)S(1)} %get-tuple-element.31), channel_id=1, source_target_pairs={{0,7},{1,2},{2,1},{3,4},{4,3},{5,6},{6,5},{7,0},{8,15},{9,10},{10,... | collective-permute-start | bytes 983048 | tf_op jit(solution)/shard_map/ppermute | solution.py:434
  19.8 0.0 collective-permute-start.7
  19.8 3.9 %second_local.1.part = f32[2,5,8,64,128]{4,3,2,1,0:T(8,128)S(1)} custom-call(f32[2,25,8,128]{3,2,1,0:T(8,128)S(1)} %get-tuple-element.19.coefs.refs_0_, f32[1]{0:T(128)S(6)} %copy.9.g0.refs_1_, f32[1]{0:T(128)S(6)} %copy.10.g1.refs_2_, f32[2,5,8,64,128]{4,3,2,1,0:T(8,128)S(1)} %get-tuple-element.20.q0, f32[2,5,8,64,128]{4,3,2,1,0:T(8,128)S(1)} %get-tuple-element.22.r1, ...), custom_call_target="tpu_custom_call" | custom-call | flops 20000000 | bytes 2600000 | tf_op jit(solution)/shard_map/second_local/pallas_call | solution.py:416
  23.7 1.9 %collective-permute-done.4.xo = f32[2,5,64,128]{3,2,1,0:T(8,128)S(1)} collective-permute-done((f32[2,5,64,128]{3,2,1,0:T(8,128)S(1)}, f32[2,5,64,128]{3,2,1,0:T(8,128)S(1)}, u32[]{:S(2)}, u32[]{:S(2)}) %collective-permute-start.4) | collective-permute-done | bytes 327712 | tf_op jit(solution)/shard_map/ppermute | solution.py:432
  25.6 0.0 collective-permute-done.5.xe
  25.6 0.0 collective-permute-done.6.yo
  25.6 0.0 collective-permute-done.7.ye
  25.6 1.6 %last_add.1 = f32[5,8,64,256]{3,2,1,0:T(8,128)} custom-call(f32[2,25,8,128]{3,2,1,0:T(8,128)S(1)} %get-tuple-element.19.coefs.refs_0_, f32[1]{0:T(128)S(6)} %copy.9.g0.refs_1_, f32[1]{0:T(128)S(6)} %copy.10.g1.refs_2_, f32[2,5,8,64,128]{4,3,2,1,0:T(8,128)S(1)} %second_local.1.part, f32[2,5,64,128]{3,2,1,0:T(8,128)S(1)} %collective-permute-done.4.xo, ...), custom_call_target="tpu_custom_call" | custom-call | flops 4000000 | bytes 2600000 | tf_op jit(solution)/shard_map/last_add/pallas_call | solution.py:416
Async XLA Ops:
  2.1 11.6 %collective-permute-start = (f32[2,5,64,128]{3,2,1,0:T(8,128)S(1)}, f32[2,5,64,128]{3,2,1,0:T(8,128)S(1)}, u32[]{:S(2)}, u32[]{:S(2)}) collective-permute-start(f32[2,5,64,128]{3,2,1,0:T(8,128)S(1)} %get-tuple-element.23), channel_id=1, source_target_pairs={{0,1},{1,0},{2,3},{3,2},{4,5},{5,4},{6,7},{7,6},{8,16},{9,17},{10,... | collective-permute-start | bytes 983048 | tf_op jit(solution)/shard_map/ppermute | solution.py:432
  5.1 9.2 %collective-permute-start.1 = (f32[2,5,64,128]{3,2,1,0:T(8,128)S(1)}, f32[2,5,64,128]{3,2,1,0:T(8,128)S(1)}, u32[]{:S(2)}, u32[]{:S(2)}) collective-permute-start(f32[2,5,64,128]{3,2,1,0:T(8,128)S(1)} %get-tuple-element.24), channel_id=1, source_target_pairs={{0,8},{8,0},{16,24},{24,16},{32,40},{40,32},{48,56},{56,48},{64,72... | collective-permute-start | bytes 983048 | tf_op jit(solution)/shard_map/ppermute | solution.py:433
  5.2 9.0 %collective-permute-start.2 = (f32[2,5,64,128]{3,2,1,0:T(8,128)S(1)}, f32[2,5,64,128]{3,2,1,0:T(8,128)S(1)}, u32[]{:S(2)}, u32[]{:S(2)}) collective-permute-start(f32[2,5,64,128]{3,2,1,0:T(8,128)S(1)} %get-tuple-element.25), channel_id=1, source_target_pairs={{0,7},{1,2},{2,1},{3,4},{4,3},{5,6},{6,5},{7,0},{8,15},{9,10},{10,... | collective-permute-start | bytes 983048 | tf_op jit(solution)/shard_map/ppermute | solution.py:434
  8.5 5.8 %collective-permute-start.3 = (f32[2,5,64,128]{3,2,1,0:T(8,128)S(1)}, f32[2,5,64,128]{3,2,1,0:T(8,128)S(1)}, u32[]{:S(2)}, u32[]{:S(2)}) collective-permute-start(f32[2,5,64,128]{3,2,1,0:T(8,128)S(1)} %get-tuple-element.26), channel_id=1, source_target_pairs={{0,1},{1,0},{2,3},{3,2},{4,5},{5,4},{6,7},{7,6},{8,9},{9,8},{10,11... | collective-permute-start | bytes 983048 | tf_op jit(solution)/shard_map/ppermute | solution.py:435
  14.6 11.0 %collective-permute-start.4 = (f32[2,5,64,128]{3,2,1,0:T(8,128)S(1)}, f32[2,5,64,128]{3,2,1,0:T(8,128)S(1)}, u32[]{:S(2)}, u32[]{:S(2)}) collective-permute-start(f32[2,5,64,128]{3,2,1,0:T(8,128)S(1)} %get-tuple-element.28), channel_id=1, source_target_pairs={{0,1},{1,0},{2,3},{3,2},{4,5},{5,4},{6,7},{7,6},{8,16},{9,17},{10,... | collective-permute-start | bytes 983048 | tf_op jit(solution)/shard_map/ppermute | solution.py:432
  17.1 8.5 %collective-permute-start.5 = (f32[2,5,64,128]{3,2,1,0:T(8,128)S(1)}, f32[2,5,64,128]{3,2,1,0:T(8,128)S(1)}, u32[]{:S(2)}, u32[]{:S(2)}) collective-permute-start(f32[2,5,64,128]{3,2,1,0:T(8,128)S(1)} %get-tuple-element.29), channel_id=1, source_target_pairs={{0,8},{8,0},{16,24},{24,16},{32,40},{40,32},{48,56},{56,48},{64,72... | collective-permute-start | bytes 983048 | tf_op jit(solution)/shard_map/ppermute | solution.py:433
  17.4 8.2 %collective-permute-start.6 = (f32[2,5,64,128]{3,2,1,0:T(8,128)S(1)}, f32[2,5,64,128]{3,2,1,0:T(8,128)S(1)}, u32[]{:S(2)}, u32[]{:S(2)}) collective-permute-start(f32[2,5,64,128]{3,2,1,0:T(8,128)S(1)} %get-tuple-element.31), channel_id=1, source_target_pairs={{0,7},{1,2},{2,1},{3,4},{4,3},{5,6},{6,5},{7,0},{8,15},{9,10},{10,... | collective-permute-start | bytes 983048 | tf_op jit(solution)/shard_map/ppermute | solution.py:434
  19.8 5.8 %collective-permute-start.7 = (f32[2,5,64,128]{3,2,1,0:T(8,128)S(1)}, f32[2,5,64,128]{3,2,1,0:T(8,128)S(1)}, u32[]{:S(2)}, u32[]{:S(2)}) collective-permute-start(f32[2,5,64,128]{3,2,1,0:T(8,128)S(1)} %get-tuple-element.32), channel_id=1, source_target_pairs={{0,1},{1,0},{2,3},{3,2},{4,5},{5,4},{6,7},{7,6},{8,9},{9,8},{10,11... | collective-permute-start | bytes 983048 | tf_op jit(solution)/shard_map/ppermute | solution.py:435

commit v5 on v4

--- a/solution.py
+++ b/solution.py
@@ -334,11 +334,38 @@
         write_faces(d, signs[d], medium(coefs, t), sums, (even, odd), t)
 
 
-def second_dom_faces(*refs):
-    *refs, weights, sums = refs
-    for t in range(TILES):
-        weights[t] = refs[0][t, pl.ds(WEIGHT, 2)]
-    second_faces(0, *refs, sums)
+def cross_terms(coefs, g1, traces, yo, ye, ready):
+    _, (sign, has) = place()
+    scale = SECTION_B1 * TIME_STEP * g1[0]
+    for t in range(TILES):
+        mask = [coefs[t, LEVEL + k] for k in range(MODES)]
+        heavy = [(m + 0.5) * mask[m] * (sign if m % 2 else 1.0) for m in range(MODES)]
+        for f in range(FIELDS):
+            other = halo_sides((ye, yo), has, t, f, mask, scale)
+            across = [
+                [sum((other[m][kind] for m in range(parity + 2, MODES, 2)), other[parity][kind]) for parity in range(2)]
+                for kind in range(2)
+            ]
+            for m in range(MODES):
+                for parity in range(2):
+                    ready[parity, t, f, rows(m), :] = (
+                        traces[parity, t, f, rows(m), :] + heavy[m] * across[m % 2][parity]
+                    )
+
+
+def second_dom_faces(coefs, g0, ready, xo, xe, even, odd, weights, sums):
+    (sign, has), _ = place()
+    scale = SECTION_B1 * TIME_STEP * g0[0]
+    for t in range(TILES):
+        weights[t] = coefs[t, pl.ds(WEIGHT, 2)]
+        mask = [coefs[t, LEVEL + k] for k in range(MODES)]
+        weight = coefs[t, WEIGHT], sign * coefs[t, WEIGHT + 1]
+        for f in range(FIELDS):
+            along = halo_sides((xe, xo), has, t, f, mask, scale)
+            for m in range(MODES):
+                for parity in range(2):
+                    sums[parity, f, rows(m), :] = ready[parity, t, f, rows(m), :] + weight[parity] * along[m][parity]
+        write_faces(0, sign, medium(coefs, t), sums, (even, odd), t)
 
 
 def second_grp_faces(weights, *refs):
@@ -481,15 +508,24 @@
         (bulk, jax.ShapeDtypeStruct((4,) + FACE, F32)),
         (LOCAL,) * 2,
         [pltpu.VMEM(BULK, F32)],
-        16_000_000,
+        20_000_000_000,
     )
     made = (coefs, g0, g1, traces, *halos)
     specs = [LOCAL, SCALAR, SCALAR] + [LOCAL] * 5
     work = [pltpu.VMEM((4,) + plane, F32)]
+    ready = call(
+        cross_terms,
+        (coefs, g1, traces, *halos[2:]),
+        [LOCAL, SCALAR] + [LOCAL] * 3,
+        jax.ShapeDtypeStruct((2,) + FACE, F32),
+        LOCAL,
+        [],
+        500_000,
+    )
     *x_faces, weights = call(
         second_dom_faces,
-        made,
-        specs,
+        (coefs, g0, ready, *halos[:2]),
+        [LOCAL, SCALAR] + [LOCAL] * 3,
         (face, face, jax.ShapeDtypeStruct((TILES, 2, MODES, LANES), F32)),
         (LOCAL,) * 3,
         work,

time: 27.5 us -> 27.5 us (level)
    ppermute x2, waiting for transfers between devices: 0.01 us -> 0.29 us  [exchange(): lax.ppermute(y_odd, 'grp', grp_perms[1])]
    pallas_call x7 -> x8, Pallas kernels: 11.5 us -> 11.5 us  [call(): pl.pallas_call(body, out_shape=outs, in_specs=specs, out_specs=out_specs,...]
  transfers between devices with their start and end apart: 8 -> 8, of which waited for: 3 -> 4; matrix products, arithmetic and copies ran while one was open for 0% -> 0% of each run, Pallas kernels for 27% -> 28%
where the time goes in v5:
time: 27.5 us; the launch traced here: 27.3 us
  Pallas kernels  11.5 us (42%)
  starting transfers between devices  11.2 us (41%)
  waiting for transfers between devices  3.23 us (12%)
  between operations  1.36 us (5%)
    pallas_call x8, Pallas kernels, call(): pl.pallas_call(body, out_shape=outs, in_specs=specs, out_specs=out_specs,...  11.5 us
    ppermute x2, starting transfers between devices, exchange(): lax.ppermute(y_odd, 'grp', grp_perms[1])  5.64 us
    ppermute x2, starting transfers between devices, exchange(): lax.ppermute(x_odd, both, dom_perms[1])  5.49 us
    ppermute x2, waiting for transfers between devices, exchange(): lax.ppermute(x_odd, both, dom_perms[1])  2.38 us
    ppermute x2, waiting for transfers between devices, exchange(): lax.ppermute(x_even, 'dom', dom_perms[0])  0.55 us
  transfers between devices with their start and end apart: 8, of which 4 were waited for; matrix products, arithmetic and copies ran while one was open for 0% of the time, Pallas kernels for 28%

profile of v5, /device:TPU:24, one launch (start us, length us, event | category | flops | bytes accessed | tf_op | source)
XLA Modules:
  0.0 27.3 jit_solution(963731744228475689)
XLA Ops:
  0.0 2.1 %first_faces.1 = (f32[2,5,8,64,128]{4,3,2,1,0:T(8,128)S(1)}, f32[2,25,8,128]{3,2,1,0:T(8,128)S(1)}, f32[4,2,5,64,128]{4,3,2,1,0:T(8,128)S(1)}, f32[2,5,64,128]{3,2,1,0:T(8,128)S(1)}, f32[2,5,64,128]{3,2,1,0:T(8,128)S(1)}) custom-call(f32[3,256]{1,0:T(4,128)} %refs_0_.1, f32[256]{0:T(256)} %refs_1_.2, f32[256]{0:T(256)} %refs_2_.2, f32[256]{0:T(256)} %refs_3_.1, ...), custom_call_target="tpu_custom_call" | custom-call | flops 2000000 | bytes 2600000 | tf_op jit(solution)/shard_map/first_faces/pallas_call | solution.py:443
  2.1 3.0 %collective-permute-start = (f32[2,5,64,128]{3,2,1,0:T(8,128)S(1)}, f32[2,5,64,128]{3,2,1,0:T(8,128)S(1)}, u32[]{:S(2)}, u32[]{:S(2)}) collective-permute-start(f32[2,5,64,128]{3,2,1,0:T(8,128)S(1)} %get-tuple-element.23), channel_id=1, source_target_pairs={{0,1},{1,0},{2,3},{3,2},{4,5},{5,4},{6,7},{7,6},{8,16},{9,17},{10,... | collective-permute-start | bytes 983048 | tf_op jit(solution)/shard_map/ppermute | solution.py:459
  5.1 0.0 collective-permute-start.1
  5.1 0.1 first_grp_faces.1
  5.2 3.2 %collective-permute-start.2 = (f32[2,5,64,128]{3,2,1,0:T(8,128)S(1)}, f32[2,5,64,128]{3,2,1,0:T(8,128)S(1)}, u32[]{:S(2)}, u32[]{:S(2)}) collective-permute-start(f32[2,5,64,128]{3,2,1,0:T(8,128)S(1)} %get-tuple-element.25), channel_id=1, source_target_pairs={{0,7},{1,2},{2,1},{3,4},{4,3},{5,6},{6,5},{7,0},{8,15},{9,10},{10,... | collective-permute-start | bytes 983048 | tf_op jit(solution)/shard_map/ppermute | solution.py:461
  8.5 0.0 collective-permute-start.3
  9.8 3.2 %local_rate.1 = (f32[2,5,8,64,128]{4,3,2,1,0:T(8,128)S(1)}, f32[4,2,5,64,128]{4,3,2,1,0:T(8,128)S(1)}) custom-call(f32[2,25,8,128]{3,2,1,0:T(8,128)S(1)} %get-tuple-element.19.coefs.refs_0_, f32[1]{0:T(128)S(6)} %copy.9.g0.refs_1_, f32[1]{0:T(128)S(6)} %copy.10.g1.refs_2_, f32[4,2,5,64,128]{4,3,2,1,0:T(8,128)S(1)} %get-tuple-element.21.sums, ...), custom_call_target="tpu_custom_call" | custom-call | flops 20000000000 | bytes 2600000 | tf_op jit(solution)/shard_map/local_rate/pallas_call | solution.py:443
  13.0 0.3 %collective-permute-done.2.yo.refs_6_ = f32[2,5,64,128]{3,2,1,0:T(8,128)S(1)} collective-permute-done((f32[2,5,64,128]{3,2,1,0:T(8,128)S(1)}, f32[2,5,64,128]{3,2,1,0:T(8,128)S(1)}, u32[]{:S(2)}, u32[]{:S(2)}) %collective-permute-start.2) | collective-permute-done | bytes 327712 | tf_op jit(solution)/shard_map/ppermute | solution.py:461
  13.2 0.0 collective-permute-done.3.ye.refs_7_
  13.2 0.1 cross_terms.1.ready
  13.4 0.3 %collective-permute-done.xo.refs_4_ = f32[2,5,64,128]{3,2,1,0:T(8,128)S(1)} collective-permute-done((f32[2,5,64,128]{3,2,1,0:T(8,128)S(1)}, f32[2,5,64,128]{3,2,1,0:T(8,128)S(1)}, u32[]{:S(2)}, u32[]{:S(2)}) %collective-permute-start) | collective-permute-done | bytes 327712 | tf_op jit(solution)/shard_map/ppermute | solution.py:459
  13.7 0.5 %collective-permute-done.1.xe.refs_5_ = f32[2,5,64,128]{3,2,1,0:T(8,128)S(1)} collective-permute-done((f32[2,5,64,128]{3,2,1,0:T(8,128)S(1)}, f32[2,5,64,128]{3,2,1,0:T(8,128)S(1)}, u32[]{:S(2)}, u32[]{:S(2)}) %collective-permute-start.1) | collective-permute-done | bytes 327712 | tf_op jit(solution)/shard_map/ppermute | solution.py:460
  14.3 0.2 second_dom_faces.1
  14.5 2.5 %collective-permute-start.4 = (f32[2,5,64,128]{3,2,1,0:T(8,128)S(1)}, f32[2,5,64,128]{3,2,1,0:T(8,128)S(1)}, u32[]{:S(2)}, u32[]{:S(2)}) collective-permute-start(f32[2,5,64,128]{3,2,1,0:T(8,128)S(1)} %get-tuple-element.28), channel_id=1, source_target_pairs={{0,1},{1,0},{2,3},{3,2},{4,5},{5,4},{6,7},{7,6},{8,16},{9,17},{10,... | collective-permute-start | bytes 983048 | tf_op jit(solution)/shard_map/ppermute | solution.py:459
  16.9 0.0 collective-permute-start.5
  16.9 0.3 %second_grp_faces.1 = (f32[2,5,64,128]{3,2,1,0:T(8,128)S(1)}, f32[2,5,64,128]{3,2,1,0:T(8,128)S(1)}) custom-call(f32[2,2,8,128]{3,2,1,0:T(8,128)S(1)} %get-tuple-element.30.weights, f32[2,25,8,128]{3,2,1,0:T(8,128)S(1)} %get-tuple-element.19.coefs.refs_0_, f32[1]{0:T(128)S(6)} %copy.9.g0.refs_1_, f32[1]{0:T(128)S(6)} %copy.10.g1.refs_2_, ...), custom_call_target="tpu_custom_call" | custom-call | flops 1000000 | bytes 2600000 | tf_op jit(solution)/shard_map/second_grp_faces/pallas_call | solution.py:443
  17.3 2.4 %collective-permute-start.6 = (f32[2,5,64,128]{3,2,1,0:T(8,128)S(1)}, f32[2,5,64,128]{3,2,1,0:T(8,128)S(1)}, u32[]{:S(2)}, u32[]{:S(2)}) collective-permute-start(f32[2,5,64,128]{3,2,1,0:T(8,128)S(1)} %get-tuple-element.31), channel_id=1, source_target_pairs={{0,7},{1,2},{2,1},{3,4},{4,3},{5,6},{6,5},{7,0},{8,15},{9,10},{10,... | collective-permute-start | bytes 983048 | tf_op jit(solution)/shard_map/ppermute | solution.py:461
  19.7 0.0 collective-permute-start.7
  19.7 3.9 %second_local.1.part = f32[2,5,8,64,128]{4,3,2,1,0:T(8,128)S(1)} custom-call(f32[2,25,8,128]{3,2,1,0:T(8,128)S(1)} %get-tuple-element.19.coefs.refs_0_, f32[1]{0:T(128)S(6)} %copy.9.g0.refs_1_, f32[1]{0:T(128)S(6)} %copy.10.g1.refs_2_, f32[2,5,8,64,128]{4,3,2,1,0:T(8,128)S(1)} %get-tuple-element.20.q0, f32[2,5,8,64,128]{4,3,2,1,0:T(8,128)S(1)} %get-tuple-element.22.r1, ...), custom_call_target="tpu_custom_call" | custom-call | flops 20000000 | bytes 2600000 | tf_op jit(solution)/shard_map/second_local/pallas_call | solution.py:443
  23.6 2.0 %collective-permute-done.4.xo = f32[2,5,64,128]{3,2,1,0:T(8,128)S(1)} collective-permute-done((f32[2,5,64,128]{3,2,1,0:T(8,128)S(1)}, f32[2,5,64,128]{3,2,1,0:T(8,128)S(1)}, u32[]{:S(2)}, u32[]{:S(2)}) %collective-permute-start.4) | collective-permute-done | bytes 327712 | tf_op jit(solution)/shard_map/ppermute | solution.py:459
  25.7 0.0 collective-permute-done.5.xe
  25.7 0.0 collective-permute-done.6.yo
  25.7 0.0 collective-permute-done.7.ye
  25.7 1.6 %last_add.1 = f32[5,8,64,256]{3,2,1,0:T(8,128)} custom-call(f32[2,25,8,128]{3,2,1,0:T(8,128)S(1)} %get-tuple-element.19.coefs.refs_0_, f32[1]{0:T(128)S(6)} %copy.9.g0.refs_1_, f32[1]{0:T(128)S(6)} %copy.10.g1.refs_2_, f32[2,5,8,64,128]{4,3,2,1,0:T(8,128)S(1)} %second_local.1.part, f32[2,5,64,128]{3,2,1,0:T(8,128)S(1)} %collective-permute-done.4.xo, ...), custom_call_target="tpu_custom_call" | custom-call | flops 4000000 | bytes 2600000 | tf_op jit(solution)/shard_map/last_add/pallas_call | solution.py:443
Async XLA Ops:
  2.1 11.6 %collective-permute-start = (f32[2,5,64,128]{3,2,1,0:T(8,128)S(1)}, f32[2,5,64,128]{3,2,1,0:T(8,128)S(1)}, u32[]{:S(2)}, u32[]{:S(2)}) collective-permute-start(f32[2,5,64,128]{3,2,1,0:T(8,128)S(1)} %get-tuple-element.23), channel_id=1, source_target_pairs={{0,1},{1,0},{2,3},{3,2},{4,5},{5,4},{6,7},{7,6},{8,16},{9,17},{10,... | collective-permute-start | bytes 983048 | tf_op jit(solution)/shard_map/ppermute | solution.py:459
  5.1 9.2 %collective-permute-start.1 = (f32[2,5,64,128]{3,2,1,0:T(8,128)S(1)}, f32[2,5,64,128]{3,2,1,0:T(8,128)S(1)}, u32[]{:S(2)}, u32[]{:S(2)}) collective-permute-start(f32[2,5,64,128]{3,2,1,0:T(8,128)S(1)} %get-tuple-element.24), channel_id=1, source_target_pairs={{0,8},{8,0},{16,24},{24,16},{32,40},{40,32},{48,56},{56,48},{64,72... | collective-permute-start | bytes 983048 | tf_op jit(solution)/shard_map/ppermute | solution.py:460
  5.2 8.0 %collective-permute-start.2 = (f32[2,5,64,128]{3,2,1,0:T(8,128)S(1)}, f32[2,5,64,128]{3,2,1,0:T(8,128)S(1)}, u32[]{:S(2)}, u32[]{:S(2)}) collective-permute-start(f32[2,5,64,128]{3,2,1,0:T(8,128)S(1)} %get-tuple-element.25), channel_id=1, source_target_pairs={{0,7},{1,2},{2,1},{3,4},{4,3},{5,6},{6,5},{7,0},{8,15},{9,10},{10,... | collective-permute-start | bytes 983048 | tf_op jit(solution)/shard_map/ppermute | solution.py:461
  8.5 4.8 %collective-permute-start.3 = (f32[2,5,64,128]{3,2,1,0:T(8,128)S(1)}, f32[2,5,64,128]{3,2,1,0:T(8,128)S(1)}, u32[]{:S(2)}, u32[]{:S(2)}) collective-permute-start(f32[2,5,64,128]{3,2,1,0:T(8,128)S(1)} %get-tuple-element.26), channel_id=1, source_target_pairs={{0,1},{1,0},{2,3},{3,2},{4,5},{5,4},{6,7},{7,6},{8,9},{9,8},{10,11... | collective-permute-start | bytes 983048 | tf_op jit(solution)/shard_map/ppermute | solution.py:462
  14.5 11.2 %collective-permute-start.4 = (f32[2,5,64,128]{3,2,1,0:T(8,128)S(1)}, f32[2,5,64,128]{3,2,1,0:T(8,128)S(1)}, u32[]{:S(2)}, u32[]{:S(2)}) collective-permute-start(f32[2,5,64,128]{3,2,1,0:T(8,128)S(1)} %get-tuple-element.28), channel_id=1, source_target_pairs={{0,1},{1,0},{2,3},{3,2},{4,5},{5,4},{6,7},{7,6},{8,16},{9,17},{10,... | collective-permute-start | bytes 983048 | tf_op jit(solution)/shard_map/ppermute | solution.py:459
  16.9 8.7 %collective-permute-start.5 = (f32[2,5,64,128]{3,2,1,0:T(8,128)S(1)}, f32[2,5,64,128]{3,2,1,0:T(8,128)S(1)}, u32[]{:S(2)}, u32[]{:S(2)}) collective-permute-start(f32[2,5,64,128]{3,2,1,0:T(8,128)S(1)} %get-tuple-element.29), channel_id=1, source_target_pairs={{0,8},{8,0},{16,24},{24,16},{32,40},{40,32},{48,56},{56,48},{64,72... | collective-permute-start | bytes 983048 | tf_op jit(solution)/shard_map/ppermute | solution.py:460
  17.3 8.4 %collective-permute-start.6 = (f32[2,5,64,128]{3,2,1,0:T(8,128)S(1)}, f32[2,5,64,128]{3,2,1,0:T(8,128)S(1)}, u32[]{:S(2)}, u32[]{:S(2)}) collective-permute-start(f32[2,5,64,128]{3,2,1,0:T(8,128)S(1)} %get-tuple-element.31), channel_id=1, source_target_pairs={{0,7},{1,2},{2,1},{3,4},{4,3},{5,6},{6,5},{7,0},{8,15},{9,10},{10,... | collective-permute-start | bytes 983048 | tf_op jit(solution)/shard_map/ppermute | solution.py:461
  19.7 6.0 %collective-permute-start.7 = (f32[2,5,64,128]{3,2,1,0:T(8,128)S(1)}, f32[2,5,64,128]{3,2,1,0:T(8,128)S(1)}, u32[]{:S(2)}, u32[]{:S(2)}) collective-permute-start(f32[2,5,64,128]{3,2,1,0:T(8,128)S(1)} %get-tuple-element.32), channel_id=1, source_target_pairs={{0,1},{1,0},{2,3},{3,2},{4,5},{5,4},{6,7},{7,6},{8,9},{9,8},{10,11... | collective-permute-start | bytes 983048 | tf_op jit(solution)/shard_map/ppermute | solution.py:462

commit v6 on v4

--- a/solution.py
+++ b/solution.py
@@ -101,12 +101,16 @@
             slots[1][t, f, rows(m), :] = two[f]
 
 
-def halo_sides(slots, has, t, f, masks, scale):
+def halo_scales(masks, has, scale):
+    other = jnp.where(has, scale, 0.0)
+    return [(scale * mask, other * mask) for mask in masks]
+
+
+def halo_sides(slots, scales, t, f):
     out = []
-    other = jnp.where(has, scale, 0.0)
-    for m in range(MODES):
-        near = (scale * masks[m]) * slots[0][t, f, rows(m), :]
-        far = (other * masks[m]) * slots[1][t, f, rows(m), :]
+    for m, (one, two) in enumerate(scales):
+        near = one * slots[0][t, f, rows(m), :]
+        far = two * slots[1][t, f, rows(m), :]
         out.append([near + far, near - far])
     return out
 
@@ -317,11 +321,10 @@
         mask = [coefs[t, LEVEL + k] for k in range(MODES)]
         live = coefs.at[t, pl.ds(WEIGHT, 2)] if table is None else table.at[t]
         weights = live[0], signs[d] * live[1]
+        scales = [halo_scales(mask, has, scale) for _, has, scale in sides]
         heavy = [(m + 0.5) * mask[m] * (signs[1 - d] if m % 2 else 1.0) for m in range(MODES)]
         for f in range(FIELDS):
-            along, other = (
-                halo_sides(slots, has, t, f, mask, scale) for slots, has, scale in (sides[d], sides[1 - d])
-            )
+            along, other = (halo_sides(sides[k][0], scales[k], t, f) for k in (d, 1 - d))
             across = [
                 [sum((other[m][kind] for m in range(parity + 2, MODES, 2)), other[parity][kind]) for parity in range(2)]
                 for kind in range(2)
@@ -345,12 +348,17 @@
     second_faces(1, *refs, weights)
 
 
-def halo_terms(coefs, t, f, sides):
+def halo_terms(coefs, t, sides):
     mask = [coefs[t, LEVEL + k] for k in range(MODES)]
     plain = [(m + 0.5) * coefs[t, LIVE + m] for m in range(MODES)]
-    first, second = (halo_sides(slots, has, t, f, mask, scale) for slots, has, scale, _ in sides)
-    weights = [[(sides[d][3] if m % 2 else 1.0) * plain[m] for m in range(MODES)] for d in range(2)]
-    return lambda a, b: weights[0][a] * first[b][a % 2] + weights[1][b] * second[a][b % 2]
+    scales = [halo_scales(mask, has, scale) for _, has, scale, _ in sides]
+    weights = [[sign * w if m % 2 else w for m, w in enumerate(plain)] for *_, sign in sides]
+
+    def of_field(f):
+        first, second = (halo_sides(sides[k][0], scales[k], t, f) for k in range(2))
+        return lambda a, b: weights[0][a] * first[b][a % 2] + weights[1][b] * second[a][b % 2]
+
+    return of_field
 
 
 def second_local(coefs, g0, g1, q0, r1, xo, xe, yo, ye, part, q1, acc):
@@ -358,9 +366,10 @@
     (sign_x, has_x), (sign_y, has_y) = place()
     sides = (((xe, xo), has_x, TIME_STEP * metric[0], sign_x), ((ye, yo), has_y, TIME_STEP * metric[1], sign_y))
     for t in range(TILES):
+        of_field = halo_terms(coefs, t, sides)
 
         def field(f, carry):
-            term = halo_terms(coefs, t, f, sides)
+            term = of_field(f)
             for a in range(MODES):
                 for b in range(MODES):
                     rate = r1[t, f, a, rows(b), :] + term(a, b)
@@ -391,8 +400,10 @@
         return pltpu.make_async_copy(done.at[t, f], out.at[f, :, :, lanes], sems.at[t, f])
 
     def tile(t, carry):
+        of_field = halo_terms(coefs, t, sides)
+
         def field(f, carry):
-            term = halo_terms(coefs, t, f, sides)
+            term = of_field(f)
             for a in range(MODES):
                 for b in range(MODES):
                     done[t, f, a, rows(b), :] = part[t, f, a, rows(b), :] + term(a, b)
@@ -431,7 +442,7 @@
     return (
         lax.ppermute(x_odd, both, dom_perms[1]),
         lax.ppermute(x_even, "dom", dom_perms[0]),
-        lax.ppermute(y_odd, "grp", grp_perms[1]),
+        lax.ppermute(y_odd, both, grp_perms[1]),
         lax.ppermute(y_even, "grp", grp_perms[0]),
     )
 
@@ -447,7 +458,16 @@
             else:
                 target = i * n_grp + (j ^ 1)
             dom_odd.append((i * n_grp + j, target))
-    grp_odd = [(j, other(j) if 0 < j < n_grp - 1 else n_grp - 1 - j) for j in range(n_grp)]
+    grp_odd = []
+    for i in range(n_dom):
+        for j in range(n_grp):
+            if 0 < j < n_grp - 1:
+                target = i * n_grp + other(j)
+            elif i % 4 in (1, 2):
+                target = (i ^ 4) * n_grp + j
+            else:
+                target = i * n_grp + n_grp - 1 - j
+            grp_odd.append((i * n_grp + j, target))
     return (even(n_dom), dom_odd), (even(n_grp), grp_odd)
 
 

time: 27.5 us -> 27.4 us (level)
  no operation moved by 1% of the time
where the time goes in v6:
time: 27.4 us; the launch traced here: 27.3 us
  Pallas kernels  11.5 us (42%)
  starting transfers between devices  11.2 us (41%)
  waiting for transfers between devices  3.23 us (12%)
  between operations  1.35 us (5%)
    pallas_call x7, Pallas kernels, call(): pl.pallas_call(body, out_shape=outs, in_specs=specs, out_specs=out_specs,...  11.5 us
    ppermute x2, starting transfers between devices, exchange(): lax.ppermute(y_odd, both, grp_perms[1])  5.64 us
    ppermute x2, starting transfers between devices, exchange(): lax.ppermute(x_odd, both, dom_perms[1])  5.5 us
    ppermute x2, waiting for transfers between devices, exchange(): lax.ppermute(x_odd, both, dom_perms[1])  2.67 us
    ppermute x2, waiting for transfers between devices, exchange(): lax.ppermute(x_even, 'dom', dom_perms[0])  0.55 us
  transfers between devices with their start and end apart: 8, of which 3 were waited for; matrix products, arithmetic and copies ran while one was open for 0% of the time, Pallas kernels for 27%

profile of v6, /device:TPU:24, one launch (start us, length us, event | category | flops | bytes accessed | tf_op | source)
XLA Modules:
  0.0 27.3 jit_solution(13599363500077451014)
XLA Ops:
  0.0 2.0 %first_faces.1 = (f32[2,5,8,64,128]{4,3,2,1,0:T(8,128)S(1)}, f32[2,25,8,128]{3,2,1,0:T(8,128)S(1)}, f32[4,2,5,64,128]{4,3,2,1,0:T(8,128)S(1)}, f32[2,5,64,128]{3,2,1,0:T(8,128)S(1)}, f32[2,5,64,128]{3,2,1,0:T(8,128)S(1)}) custom-call(f32[3,256]{1,0:T(4,128)} %refs_0_.1, f32[256]{0:T(256)} %refs_1_.3, f32[256]{0:T(256)} %refs_2_.3, f32[256]{0:T(256)} %refs_3_.1, ...), custom_call_target="tpu_custom_call" | custom-call | flops 2000000 | bytes 2600000 | tf_op jit(solution)/shard_map/first_faces/pallas_call | solution.py:427
  2.1 3.0 %collective-permute-start = (f32[2,5,64,128]{3,2,1,0:T(8,128)S(1)}, f32[2,5,64,128]{3,2,1,0:T(8,128)S(1)}, u32[]{:S(2)}, u32[]{:S(2)}) collective-permute-start(f32[2,5,64,128]{3,2,1,0:T(8,128)S(1)} %get-tuple-element.23), channel_id=1, source_target_pairs={{0,1},{1,0},{2,3},{3,2},{4,5},{5,4},{6,7},{7,6},{8,16},{9,17},{10,... | collective-permute-start | bytes 983048 | tf_op jit(solution)/shard_map/ppermute | solution.py:443
  5.1 0.0 collective-permute-start.1
  5.1 0.1 first_grp_faces.1
  5.2 3.2 %collective-permute-start.2 = (f32[2,5,64,128]{3,2,1,0:T(8,128)S(1)}, f32[2,5,64,128]{3,2,1,0:T(8,128)S(1)}, u32[]{:S(2)}, u32[]{:S(2)}) collective-permute-start(f32[2,5,64,128]{3,2,1,0:T(8,128)S(1)} %get-tuple-element.25), channel_id=1, source_target_pairs={{0,7},{1,2},{2,1},{3,4},{4,3},{5,6},{6,5},{7,0},{8,40},{9,10},{10,... | collective-permute-start | bytes 983048 | tf_op jit(solution)/shard_map/ppermute | solution.py:445
  8.5 0.0 collective-permute-start.3
  9.8 3.1 %local_rate.1 = (f32[2,5,8,64,128]{4,3,2,1,0:T(8,128)S(1)}, f32[4,2,5,64,128]{4,3,2,1,0:T(8,128)S(1)}) custom-call(f32[2,25,8,128]{3,2,1,0:T(8,128)S(1)} %get-tuple-element.19.coefs.refs_0_, f32[1]{0:T(128)S(6)} %copy.9.g0.refs_1_, f32[1]{0:T(128)S(6)} %copy.10.g1.refs_2_, f32[4,2,5,64,128]{4,3,2,1,0:T(8,128)S(1)} %get-tuple-element.21.sums, ...), custom_call_target="tpu_custom_call" | custom-call | flops 16000000 | bytes 2600000 | tf_op jit(solution)/shard_map/local_rate/pallas_call | solution.py:427
  12.9 0.8 %collective-permute-done.xo.refs_4_ = f32[2,5,64,128]{3,2,1,0:T(8,128)S(1)} collective-permute-done((f32[2,5,64,128]{3,2,1,0:T(8,128)S(1)}, f32[2,5,64,128]{3,2,1,0:T(8,128)S(1)}, u32[]{:S(2)}, u32[]{:S(2)}) %collective-permute-start) | collective-permute-done | bytes 327712 | tf_op jit(solution)/shard_map/ppermute | solution.py:443
  13.7 0.5 %collective-permute-done.1.xe.refs_5_ = f32[2,5,64,128]{3,2,1,0:T(8,128)S(1)} collective-permute-done((f32[2,5,64,128]{3,2,1,0:T(8,128)S(1)}, f32[2,5,64,128]{3,2,1,0:T(8,128)S(1)}, u32[]{:S(2)}, u32[]{:S(2)}) %collective-permute-start.1) | collective-permute-done | bytes 327712 | tf_op jit(solution)/shard_map/ppermute | solution.py:444
  14.2 0.0 collective-permute-done.2.yo.refs_6_
  14.2 0.0 collective-permute-done.3.ye.refs_7_
  14.3 0.3 %second_dom_faces.1 = (f32[2,5,64,128]{3,2,1,0:T(8,128)S(1)}, f32[2,5,64,128]{3,2,1,0:T(8,128)S(1)}, f32[2,2,8,128]{3,2,1,0:T(8,128)S(1)}) custom-call(f32[2,25,8,128]{3,2,1,0:T(8,128)S(1)} %get-tuple-element.19.coefs.refs_0_, f32[1]{0:T(128)S(6)} %copy.9.g0.refs_1_, f32[1]{0:T(128)S(6)} %copy.10.g1.refs_2_, ...), custom_call_target="tpu_custom_call" | custom-call | flops 1000000 | bytes 2600000 | tf_op jit(solution)/shard_map/second_dom_faces/pallas_call | solution.py:427
  14.6 2.5 %collective-permute-start.4 = (f32[2,5,64,128]{3,2,1,0:T(8,128)S(1)}, f32[2,5,64,128]{3,2,1,0:T(8,128)S(1)}, u32[]{:S(2)}, u32[]{:S(2)}) collective-permute-start(f32[2,5,64,128]{3,2,1,0:T(8,128)S(1)} %get-tuple-element.28), channel_id=1, source_target_pairs={{0,1},{1,0},{2,3},{3,2},{4,5},{5,4},{6,7},{7,6},{8,16},{9,17},{10,... | collective-permute-start | bytes 983048 | tf_op jit(solution)/shard_map/ppermute | solution.py:443
  17.1 0.0 collective-permute-start.5
  17.1 0.3 %second_grp_faces.1 = (f32[2,5,64,128]{3,2,1,0:T(8,128)S(1)}, f32[2,5,64,128]{3,2,1,0:T(8,128)S(1)}) custom-call(f32[2,2,8,128]{3,2,1,0:T(8,128)S(1)} %get-tuple-element.30.weights, f32[2,25,8,128]{3,2,1,0:T(8,128)S(1)} %get-tuple-element.19.coefs.refs_0_, f32[1]{0:T(128)S(6)} %copy.9.g0.refs_1_, f32[1]{0:T(128)S(6)} %copy.10.g1.refs_2_, ...), custom_call_target="tpu_custom_call" | custom-call | flops 1000000 | bytes 2600000 | tf_op jit(solution)/shard_map/second_grp_faces/pallas_call | solution.py:427
  17.4 2.4 %collective-permute-start.6 = (f32[2,5,64,128]{3,2,1,0:T(8,128)S(1)}, f32[2,5,64,128]{3,2,1,0:T(8,128)S(1)}, u32[]{:S(2)}, u32[]{:S(2)}) collective-permute-start(f32[2,5,64,128]{3,2,1,0:T(8,128)S(1)} %get-tuple-element.31), channel_id=1, source_target_pairs={{0,7},{1,2},{2,1},{3,4},{4,3},{5,6},{6,5},{7,0},{8,40},{9,10},{10,... | collective-permute-start | bytes 983048 | tf_op jit(solution)/shard_map/ppermute | solution.py:445
  19.8 0.0 collective-permute-start.7
  19.8 3.9 %second_local.1.part = f32[2,5,8,64,128]{4,3,2,1,0:T(8,128)S(1)} custom-call(f32[2,25,8,128]{3,2,1,0:T(8,128)S(1)} %get-tuple-element.19.coefs.refs_0_, f32[1]{0:T(128)S(6)} %copy.9.g0.refs_1_, f32[1]{0:T(128)S(6)} %copy.10.g1.refs_2_, f32[2,5,8,64,128]{4,3,2,1,0:T(8,128)S(1)} %get-tuple-element.20.q0, f32[2,5,8,64,128]{4,3,2,1,0:T(8,128)S(1)} %get-tuple-element.22.r1, ...), custom_call_target="tpu_custom_call" | custom-call | flops 20000000 | bytes 2600000 | tf_op jit(solution)/shard_map/second_local/pallas_call | solution.py:427
  23.7 1.9 %collective-permute-done.4.xo = f32[2,5,64,128]{3,2,1,0:T(8,128)S(1)} collective-permute-done((f32[2,5,64,128]{3,2,1,0:T(8,128)S(1)}, f32[2,5,64,128]{3,2,1,0:T(8,128)S(1)}, u32[]{:S(2)}, u32[]{:S(2)}) %collective-permute-start.4) | collective-permute-done | bytes 327712 | tf_op jit(solution)/shard_map/ppermute | solution.py:443
  25.6 0.0 collective-permute-done.5.xe
  25.6 0.0 collective-permute-done.6.yo
  25.6 0.0 collective-permute-done.7.ye
  25.6 1.7 %last_add.1 = f32[5,8,64,256]{3,2,1,0:T(8,128)} custom-call(f32[2,25,8,128]{3,2,1,0:T(8,128)S(1)} %get-tuple-element.19.coefs.refs_0_, f32[1]{0:T(128)S(6)} %copy.9.g0.refs_1_, f32[1]{0:T(128)S(6)} %copy.10.g1.refs_2_, f32[2,5,8,64,128]{4,3,2,1,0:T(8,128)S(1)} %second_local.1.part, f32[2,5,64,128]{3,2,1,0:T(8,128)S(1)} %collective-permute-done.4.xo, ...), custom_call_target="tpu_custom_call" | custom-call | flops 4000000 | bytes 2600000 | tf_op jit(solution)/shard_map/last_add/pallas_call | solution.py:427
Async XLA Ops:
  2.1 11.6 %collective-permute-start = (f32[2,5,64,128]{3,2,1,0:T(8,128)S(1)}, f32[2,5,64,128]{3,2,1,0:T(8,128)S(1)}, u32[]{:S(2)}, u32[]{:S(2)}) collective-permute-start(f32[2,5,64,128]{3,2,1,0:T(8,128)S(1)} %get-tuple-element.23), channel_id=1, source_target_pairs={{0,1},{1,0},{2,3},{3,2},{4,5},{5,4},{6,7},{7,6},{8,16},{9,17},{10,... | collective-permute-start | bytes 983048 | tf_op jit(solution)/shard_map/ppermute | solution.py:443
  5.1 9.2 %collective-permute-start.1 = (f32[2,5,64,128]{3,2,1,0:T(8,128)S(1)}, f32[2,5,64,128]{3,2,1,0:T(8,128)S(1)}, u32[]{:S(2)}, u32[]{:S(2)}) collective-permute-start(f32[2,5,64,128]{3,2,1,0:T(8,128)S(1)} %get-tuple-element.24), channel_id=1, source_target_pairs={{0,8},{8,0},{16,24},{24,16},{32,40},{40,32},{48,56},{56,48},{64,72... | collective-permute-start | bytes 983048 | tf_op jit(solution)/shard_map/ppermute | solution.py:444
  5.2 9.0 %collective-permute-start.2 = (f32[2,5,64,128]{3,2,1,0:T(8,128)S(1)}, f32[2,5,64,128]{3,2,1,0:T(8,128)S(1)}, u32[]{:S(2)}, u32[]{:S(2)}) collective-permute-start(f32[2,5,64,128]{3,2,1,0:T(8,128)S(1)} %get-tuple-element.25), channel_id=1, source_target_pairs={{0,7},{1,2},{2,1},{3,4},{4,3},{5,6},{6,5},{7,0},{8,40},{9,10},{10,... | collective-permute-start | bytes 983048 | tf_op jit(solution)/shard_map/ppermute | solution.py:445
  8.5 5.8 %collective-permute-start.3 = (f32[2,5,64,128]{3,2,1,0:T(8,128)S(1)}, f32[2,5,64,128]{3,2,1,0:T(8,128)S(1)}, u32[]{:S(2)}, u32[]{:S(2)}) collective-permute-start(f32[2,5,64,128]{3,2,1,0:T(8,128)S(1)} %get-tuple-element.26), channel_id=1, source_target_pairs={{0,1},{1,0},{2,3},{3,2},{4,5},{5,4},{6,7},{7,6},{8,9},{9,8},{10,11... | collective-permute-start | bytes 983048 | tf_op jit(solution)/shard_map/ppermute | solution.py:446
  14.6 11.0 %collective-permute-start.4 = (f32[2,5,64,128]{3,2,1,0:T(8,128)S(1)}, f32[2,5,64,128]{3,2,1,0:T(8,128)S(1)}, u32[]{:S(2)}, u32[]{:S(2)}) collective-permute-start(f32[2,5,64,128]{3,2,1,0:T(8,128)S(1)} %get-tuple-element.28), channel_id=1, source_target_pairs={{0,1},{1,0},{2,3},{3,2},{4,5},{5,4},{6,7},{7,6},{8,16},{9,17},{10,... | collective-permute-start | bytes 983048 | tf_op jit(solution)/shard_map/ppermute | solution.py:443
  17.1 8.5 %collective-permute-start.5 = (f32[2,5,64,128]{3,2,1,0:T(8,128)S(1)}, f32[2,5,64,128]{3,2,1,0:T(8,128)S(1)}, u32[]{:S(2)}, u32[]{:S(2)}) collective-permute-start(f32[2,5,64,128]{3,2,1,0:T(8,128)S(1)} %get-tuple-element.29), channel_id=1, source_target_pairs={{0,8},{8,0},{16,24},{24,16},{32,40},{40,32},{48,56},{56,48},{64,72... | collective-permute-start | bytes 983048 | tf_op jit(solution)/shard_map/ppermute | solution.py:444
  17.4 8.2 %collective-permute-start.6 = (f32[2,5,64,128]{3,2,1,0:T(8,128)S(1)}, f32[2,5,64,128]{3,2,1,0:T(8,128)S(1)}, u32[]{:S(2)}, u32[]{:S(2)}) collective-permute-start(f32[2,5,64,128]{3,2,1,0:T(8,128)S(1)} %get-tuple-element.31), channel_id=1, source_target_pairs={{0,7},{1,2},{2,1},{3,4},{4,3},{5,6},{6,5},{7,0},{8,40},{9,10},{10,... | collective-permute-start | bytes 983048 | tf_op jit(solution)/shard_map/ppermute | solution.py:445
  19.8 5.8 %collective-permute-start.7 = (f32[2,5,64,128]{3,2,1,0:T(8,128)S(1)}, f32[2,5,64,128]{3,2,1,0:T(8,128)S(1)}, u32[]{:S(2)}, u32[]{:S(2)}) collective-permute-start(f32[2,5,64,128]{3,2,1,0:T(8,128)S(1)} %get-tuple-element.32), channel_id=1, source_target_pairs={{0,1},{1,0},{2,3},{3,2},{4,5},{5,4},{6,7},{7,6},{8,9},{9,8},{10,11... | collective-permute-start | bytes 983048 | tf_op jit(solution)/shard_map/ppermute | solution.py:446
